TPU v7x, 512 devices: a whole 4x8x8 slice. The times are simulated.
512 devices in a mesh: tile: 32 (over z, x_lo, core), src: 16 (over x_hi, y).
Axes of the slice: x: 4 (x_hi: 2, x_lo: 2; x = x_hi * 2 + x_lo), y: 8, z: 8, core: 2. Of those that a mesh axis runs over, the one named last changes fastest.
Arguments:
- mask: float32 [256, 8192], P('src', 'tile'), may hold values from 0 to 1
- target: int32 [256, 8192], P(None, 'tile'), may hold values 0 or 1
- shifts: int32 [128, 2], P('src'), may hold values from -12 to 12
- weights: float32 [128], P('src'), may hold values from 0.5 to 2
Outputs:
- resist: float32 [256, 8192], P('src', 'tile')
- mask_grad: float32 [256, 8192], P('src', 'tile')
- source_grad: float32 [128], P('src')
All inputs are finite; a program needn't handle non-finite values. No bound on the sum of `target` on one device may be relied on, other than what follows from the above.
Results may differ from a plain program's by a relative error of at most 0.0003.
Values sent between devices are 32-bit elements; how exact they have to be, the bound alone decides.
A program may use at most 64 MiB of HBM per device.

v0:
```python
import jax
import jax.numpy as jnp
from jax import lax
from jax.sharding import PartitionSpec as P

TILE = 256
MARGIN = 32
BAND = 64
RAD = 16
EXT = 320


STEEP = 8.0
THRESH = 0.25
LOSS_SCALE = 2.0


def with_halo(cells, sides, width):
    for axis, dim in sides:
        count = lax.axis_size(axis)
        ends = count - 1
        head = lax.slice_in_dim(cells, 0, width, axis=dim)
        tail = lax.slice_in_dim(cells, cells.shape[dim] - width, cells.shape[dim], axis=dim)
        cells = jnp.concatenate(
            [
                lax.ppermute(tail, axis, [(i, (i + 1) % count) for i in range(ends)]),
                cells,
                lax.ppermute(head, axis, [((i + 1) % count, i) for i in range(ends)]),
            ],
            axis=dim,
        )
    return cells


def product(left, right):
    return jnp.matmul(left, right, precision=lax.Precision.HIGHEST)


def tables():
    freq = jnp.arange(BAND, dtype=jnp.int32) - BAND // 2
    place = jnp.arange(EXT, dtype=jnp.int32)
    phase = (freq[:, None] * place[None, :] % EXT).astype(jnp.float32) * (2.0 * jnp.pi / EXT)
    fwd_real = jnp.cos(phase) / EXT
    fwd_imag = -jnp.sin(phase) / EXT
    inner = place[MARGIN : MARGIN + TILE]
    phase_back = (inner[:, None] * freq[None, :] % EXT).astype(jnp.float32) * (2.0 * jnp.pi / EXT)
    return (fwd_real, fwd_imag, jnp.cos(phase_back), jnp.sin(phase_back), freq)


def pupils(shifts, freq):
    rows_off = freq[None, :, None] + shifts[:, 0][:, None, None]
    cols_off = freq[None, None, :] + shifts[:, 1][:, None, None]
    return (rows_off * rows_off + cols_off * cols_off <= RAD * RAD).astype(jnp.float32)


def make_fields(left_r, left_i, right_r, right_i, spec_real, spec_imag, pupil):
    band_real = pupil * spec_real
    band_imag = pupil * spec_imag
    mid_real = product(left_r, band_real) - product(left_i, band_imag)
    mid_imag = product(left_r, band_imag) + product(left_i, band_real)
    field_real = product(mid_real, right_r.T) - product(mid_imag, right_i.T)
    field_imag = product(mid_real, right_i.T) + product(mid_imag, right_r.T)
    return (field_real, field_imag)


def band_grads(left_r, left_i, right_r, right_i, adj_real, adj_imag, pupil):
    back_real = product(left_r.T, adj_real) + product(left_i.T, adj_imag)
    back_imag = product(left_r.T, adj_imag) - product(left_i.T, adj_real)
    dband_real = product(back_real, right_r) + product(back_imag, right_i)
    dband_imag = product(back_imag, right_r) - product(back_real, right_i)
    return (jnp.sum(pupil * dband_real, axis=0), jnp.sum(pupil * dband_imag, axis=0))


def local(mask, target, shifts, weights):
    rows = mask.shape[0]
    per_dev = weights.shape[0]
    sources = per_dev * lax.axis_size("src")
    tiles = lax.axis_size("tile")
    fwd_real, fwd_imag, inv_real, inv_imag, freq = tables()
    ext_rows = with_halo(mask, (("tile", 1),), MARGIN)
    piece = lax.all_gather(ext_rows, "src", axis=0, tiled=True)
    cols_real = lax.dynamic_slice_in_dim(fwd_real, MARGIN, piece.shape[0], 1)
    cols_imag = lax.dynamic_slice_in_dim(fwd_imag, MARGIN, piece.shape[0], 1)
    half_real = product(cols_real, piece)
    half_imag = product(cols_imag, piece)
    next_real = product(half_real, fwd_real.T) - product(half_imag, fwd_imag.T)
    next_imag = product(half_real, fwd_imag.T) + product(half_imag, fwd_real.T)
    own_first = lax.axis_index("src") * rows
    goal_all = target.astype(jnp.float32)
    norm = sources * (tiles * TILE * TILE)
    pupil = pupils(shifts, freq)
    field_real, field_imag = make_fields(
        inv_real, inv_imag, inv_real, inv_imag, next_real, next_imag, pupil
    )
    power = field_real * field_real + field_imag * field_imag
    scaled = weights / sources
    partial_value = jnp.sum(scaled[:, None, None] * power, axis=0)
    image = lax.psum(partial_value, "src")
    printed = jax.nn.sigmoid(STEEP * (image - THRESH))
    slope = LOSS_SCALE * 2.0 * (printed - goal_all) * STEEP * printed * (1.0 - printed)
    factor = (2.0 * scaled)[:, None, None] * slope
    local_real, local_imag = band_grads(
        inv_real, inv_imag, inv_real, inv_imag, factor * field_real, factor * field_imag, pupil
    )
    weight_part = jnp.sum(slope[None, :, :] * power, axis=(1, 2)) / norm
    resist = lax.dynamic_slice_in_dim(printed, own_first, rows, 0)
    grad_real, grad_imag = lax.psum((local_real, local_imag), "src")
    inner_real = fwd_real[:, MARGIN : MARGIN + TILE]
    inner_imag = fwd_imag[:, MARGIN : MARGIN + TILE]
    right_real = product(grad_real, inner_real) + product(grad_imag, inner_imag)
    right_imag = product(grad_imag, inner_real) - product(grad_real, inner_imag)
    own_rows = MARGIN + own_first
    mine_real = lax.dynamic_slice_in_dim(fwd_real, own_rows, rows, 1)
    mine_imag = lax.dynamic_slice_in_dim(fwd_imag, own_rows, rows, 1)
    mask_grad = product(mine_real.T, right_real) + product(mine_imag.T, right_imag)
    source_grad = lax.psum(weight_part, "tile")
    return (resist, mask_grad, source_grad)


def solution(mesh):
    placed = (P("src", "tile"), P(None, "tile"), P("src", None), P("src"))
    return jax.shard_map(
        local,
        mesh=mesh,
        in_specs=placed,
        out_specs=(P("src", "tile"), P("src", "tile"), P("src")),
        check_vma=False,
    )
```

profile of v0, /device:TPU:4, one launch (start us, length us, event | category | flops | bytes accessed | tf_op | source)
XLA Modules:
  0.0 393.1 jit_solution(12828506551048408955)
XLA Ops:
  7.2 0.8 fusion.223
  8.0 1.7 collective-permute-start
  9.7 1.3 collective-permute-start.1
  11.5 0.8 slice_bitcast_fusion.1
  13.8 0.8 pad_maximum_fusion
  14.6 41.5 %all_gather.3 = f32[256,320]{1,0:T(8,128)S(1)} all-gather(f32[16,320]{1,0:T(8,128)S(1)} %pad_maximum_fusion), channel_id=1, replica_groups=mesh['tile'=32,'src'=16] {'src'}, dimensions={0}, use_global_device_ids=true | all-gather | bytes 348160 | tf_op jit(solution)/shard_map/all_gather | solution.py:81
  57.2 0.7 fusion.89
  58.3 0.7 convolution_subtract_fusion.3
  59.0 0.7 convolution_add_fusion.3
  60.0 0.9 fusion.75
  60.9 0.9 fusion.62
  61.9 0.9 fusion.65
  62.8 0.9 fusion.73
  63.7 2.1 fusion.24
  65.8 2.1 fusion.22
  68.0 2.3 convolution_subtract_fusion
  70.3 4.6 %multiply_reduce_fusion.1 = (f32[256,256]{1,0:T(8,128)}, f32[8,256,256]{2,1,0:T(8,128)}) fusion(f32[8]{0:T(128)S(1)} %get-tuple-element.14, f32[8,256,256]{2,1,0:T(8,128)S(1)} %convolution_subtract_fusion, f32[8,256,256]{2,1,0:T(8,128)S(1)} %fusion.22, s32[64]{0:T(128)S(1)} %iota_add_fusion, s32[256]{0:T(256)S(1)} %slice.49, f32[256,8,64]{0,2,1:T(8,128)S(1)} %bitcast.83, ...), kind=kOutput, calls=%fused_computation.3 | convolution fusion | flops 406011904 | bytes 7603488 | tf_op jit(solution)/shard_map/dot_general | solution.py:36
  74.9 161.6 %all-reduce.3.cloned.1.call-done = f32[256,256]{1,0:T(8,128)} async-done(((f32[256,256]{1,0:T(8,128)}), f32[256,256]{1,0:T(8,128)}) %all-reduce.3.cloned.1.call-update) | async-done | bytes 262160 | tf_op jit(solution)/shard_map/psum | solution.py:98
  236.5 1.8 subtract_multiply_fusion
  238.2 2.1 multiply_reduce_fusion
  240.3 1.8 fusion
  242.1 1.8 fusion.1
  244.0 54.2 %psum.31 = f32[8]{0:T(128)} all-reduce(f32[8]{0:T(128)S(1)} %broadcast_multiply_fusion), channel_id=1, replica_groups=mesh['tile'=32,'src'=16] {'tile'}, use_global_device_ids=true, to_apply=%region_7.8 | all-reduce | flops 8 | bytes 64 | tf_op jit(solution)/shard_map/psum | solution.py:116
  298.2 3.6 fusion.7
  301.8 0.9 fusion.45
  302.7 1.8 fusion.5
  304.5 0.9 fusion.48
  305.4 0.9 fusion.10
  306.3 0.9 fusion.11
  307.2 75.4 %all-reduce = (f32[64,64]{1,0:T(8,128)S(1)}, f32[64,64]{1,0:T(8,128)S(1)}) all-reduce(f32[64,64]{1,0:T(8,128)S(1)} %fusion.11, f32[64,64]{1,0:T(8,128)S(1)} %fusion.10), channel_id=1, replica_groups=mesh['tile'=32,'src'=16] {'src'}, use_global_device_ids=true, to_apply=%region_3.4 | all-reduce | flops 8192 | bytes 65536 | tf_op jit(solution)/shard_map/psum | solution.py:107
  384.1 0.9 convolution_add_fusion.4
  385.0 1.3 constant_dynamic-slice_fusion
  (30 shorter events, 5.2 us)
Async XLA Ops:
  7.2 229.3 %all-reduce.3.cloned.1.call-start = ((), (), s32[]{:S(2)}) async-start(), calls=%async_computation | async-start | bytes 524288 | tf_op jit(solution)/shard_map/psum | solution.py:98
  8.0 5.1 %collective-permute-start = (f32[16,32]{1,0:T(8,128)S(1)}, f32[16,32]{1,0:T(8,128)S(1)}, u32[]{:S(2)}, u32[]{:S(2)}) collective-permute-start(f32[16,32]{1,0:T(8,128)S(1)} %get-tuple-element.7), channel_id=1, source_target_pairs={{0,16},{16,32},{32,48},{48,64},{64,80},{80,96},{96,112},{112,128},... | collective-permute-start | bytes 6152 | tf_op jit(solution)/shard_map/ppermute | solution.py:26
  9.7 4.1 %collective-permute-start.1 = (f32[16,32]{1,0:T(8,128)S(1)}, f32[16,32]{1,0:T(8,128)S(1)}, u32[]{:S(2)}, u32[]{:S(2)}) collective-permute-start(f32[16,32]{1,0:T(8,128)S(1)} %get-tuple-element.8), channel_id=1, source_target_pairs={{16,0},{32,16},{48,32},{64,48},{80,64},{96,80},{112,96},{128,112},... | collective-permute-start | bytes 6152 | tf_op jit(solution)/shard_map/ppermute | solution.py:28
  11.5 48.3 %copy-start.1 = (f32[64,320]{1,0:T(8,128)}, f32[64,320]{1,0:T(8,128)S(1)}, u32[]{:S(2)}) copy-start(f32[64,320]{1,0:T(8,128)S(1)} %get-tuple-element.18) | copy-start | bytes 245764
  70.3 166.2 %copy-start.3 = (s32[256,256]{1,0:T(8,128)S(1)}, s32[256,256]{1,0:T(8,128)}, u32[]{:S(2)}) copy-start(s32[256,256]{1,0:T(8,128)} %param.5) | copy-start | bytes 786436
  298.2 4.5 %copy-start = (f32[8,256,256]{2,1,0:T(8,128)S(1)}, f32[8,256,256]{2,1,0:T(8,128)}, u32[]{:S(2)}) copy-start(f32[8,256,256]{2,1,0:T(8,128)} %get-tuple-element.20) | copy-start | bytes 6291460
  304.5 78.1 %copy-start.2 = (f32[64,320]{1,0:T(8,128)S(1)}, f32[64,320]{1,0:T(8,128)}, u32[]{:S(2)}) copy-start(f32[64,320]{1,0:T(8,128)} %copy-done.1) | copy-start | bytes 245764
Sparse Core Ops, SparseCore 0:
  75.0 161.4 all-reduce.2
where the time goes:
time: 394 us; the launch traced here: 393 us
  blocking collectives  171 us (43%)
  waiting for transfers between devices  162 us (41%)
  matrix products  33.1 us (8%)
  between operations  14.3 us (4%)
  other arithmetic  6 us (2%)
    psum x1, waiting for transfers between devices, local(): image = lax.psum(partial_value, 'src')  162 us
    psum x1, blocking collectives, local(): grad_real, grad_imag = lax.psum((local_real, local_imag), 'src')  75.4 us
    psum x1, blocking collectives, local(): source_grad = lax.psum(weight_part, 'tile')  54.2 us
    all_gather x1, blocking collectives, local(): piece = lax.all_gather(ext_rows, 'src', axis=0, tiled=True)  41.5 us
    dot_general x24, matrix products, product(): return jnp.matmul(left, right, precision=lax.Precision.HIGHEST)  29.6 us
  transfers between devices with their start and end apart: 3, of which 2 were waited for; matrix products, arithmetic and copies ran while one was open for 1% of the time, Pallas kernels for 0%

commit v1 on v0

v1 whole, which is shorter than its diff:
```python
import functools

import jax
import jax.numpy as jnp
import ml_dtypes
import numpy as np
from jax import lax
from jax.experimental import pallas as pl
from jax.experimental.pallas import tpu as pltpu
from jax.sharding import PartitionSpec as P

TILE = 256
MARGIN = 32
BAND = 64
RAD = 16
EXT = 320
STEEP = 8.0
THRESH = 0.25
LOSS_SCALE = 2.0

N_SRC = 16
N_TILE = 32
PER_DEV = 8
SOURCES = 128
ROWS = 16
HALF = 32
ROWS_C = 80
COLS_C = 128
QUAD = 4
GROUP = 4
DEPTH = 8

MESH = pl.DeviceIdType.MESH
BF16 = ml_dtypes.bfloat16


def halves(table):
    high = table.astype(BF16)
    low = (table - high.astype(np.float64)).astype(BF16)
    return high, low


def column_slots():
    plus = np.arange(HALF)
    return np.concatenate([plus, -plus]), np.concatenate([np.ones(HALF), [0.0], np.ones(HALF - 1)])


def waves(freq, place, period):
    phase = 2.0 * np.pi * ((freq[:, None] * place[None, :]) % period) / period
    return np.cos(phase), np.sin(phase)


def interpolation(points):
    order = np.arange(-2 * RAD, 2 * RAD + 1)
    place = np.arange(TILE) + MARGIN
    offset = place[:, None] / EXT - np.arange(points)[None, :] / points
    return np.cos(2.0 * np.pi * order[None, None, :] * offset[:, :, None]).sum(axis=2) / points


def build_tables():
    slots, used = column_slots()
    row_freq = np.arange(BAND) - BAND // 2
    pixels = np.arange(TILE) + MARGIN
    parts = {}

    real, imag = waves(np.arange(HALF), np.arange(EXT), EXT)
    fwd = np.concatenate([real, -imag], axis=0).T / EXT
    wide = np.zeros((2 * TILE, 2 * HALF))
    wide[:TILE] = fwd[MARGIN : MARGIN + TILE]
    wide[TILE + 96 : TILE + 128] = fwd[:MARGIN]
    wide[TILE + 128 : TILE + 160] = fwd[MARGIN + TILE :]
    high, low = halves(np.concatenate([wide, wide], axis=1))
    parts["enter"] = np.concatenate([high, low], axis=1)

    rows = np.arange(TILE).reshape(N_SRC, 2, 8)
    first, second = rows[:, 0].reshape(-1), rows[:, 1].reshape(-1)
    real, imag = waves(row_freq, pixels, EXT)
    real, imag = real / EXT, -imag / EXT
    both = np.concatenate([real, imag], axis=0)
    high, low = halves(np.concatenate([both[:, first], both[:, second]], axis=0))
    parts["spec"] = np.concatenate([high, high], axis=1)
    spec_low = low

    inter_rows, inter_cols = 2.0 * interpolation(ROWS_C), interpolation(COLS_C)
    even, odd = np.arange(0, COLS_C, 2), np.arange(1, COLS_C, 2)
    for name, order in (("even", np.concatenate([even, odd])), ("odd", np.concatenate([odd, even]))):
        real, imag = waves(slots, order, COLS_C)
        real, imag = real * used[:, None], imag * used[:, None]
        cols = np.concatenate(
            [np.concatenate([real, imag], axis=1), np.concatenate([-imag, real], axis=1)], axis=0
        )
        high, low = halves(cols)
        parts["cols_" + name] = np.concatenate([high, high], axis=0)
        parts["cols_low_" + name] = low
        high, low = halves(np.concatenate([cols[:, :COLS_C].T, cols[:, COLS_C:].T], axis=0))
        parts["cols_back_" + name] = np.concatenate([high, low], axis=1)

    lows = []
    for name, start in (("even", 0), ("odd", 1)):
        real, imag = waves(row_freq, np.arange(start, ROWS_C, 2), ROWS_C)
        real, imag = real.T, imag.T
        high, low = halves(
            np.concatenate(
                [np.concatenate([real, -imag], axis=1), np.concatenate([imag, real], axis=1)], axis=0
            )
        )
        parts["rows_" + name] = np.concatenate([high, high], axis=1)
        lows.append(low)
        pad = np.zeros((2 * BAND, TILE - 3 * ROWS_C), BF16)
        parts["rows_back_" + name] = np.concatenate([high.T, high.T, low.T, pad], axis=1)
    rows_low = np.concatenate(lows, axis=0)

    mixed = np.concatenate([np.arange(0, ROWS_C, 2), np.arange(1, ROWS_C, 2)])
    inter_rows, inter_cols = inter_rows[:, mixed], inter_cols[:, np.concatenate([even, odd])]
    high, low = halves(inter_rows)
    pad = np.zeros((TILE, TILE - 3 * ROWS_C), BF16)
    parts["fine_rows"] = np.concatenate([high, high, low, pad], axis=1)
    high, low = halves(inter_cols.T)
    parts["fine_cols"] = np.concatenate([high, high], axis=0)
    parts["fine_cols_low"] = low
    parts["coarse_cols"] = np.concatenate([high.T, low.T], axis=1)
    high, low = halves(inter_rows.T)
    parts["coarse_rows"] = high
    parts["coarse_rows_low"] = low

    high, low = halves(np.concatenate([both[:, first], both[:, second]], axis=1).T)
    parts["leave"] = np.concatenate([high, high], axis=1)
    leave_low = low
    last = fwd[MARGIN : MARGIN + TILE].T
    high, low = halves(np.concatenate([last, last], axis=0))
    parts["last"] = high
    parts["last_low"] = low

    parts["lows_a"] = np.concatenate([spec_low, np.zeros((TILE, 128), BF16)], axis=1)
    rows_low = np.concatenate([rows_low, np.zeros((TILE - 2 * ROWS_C, 128), BF16)], axis=0)
    parts["lows_b"] = np.concatenate([leave_low, rows_low], axis=1)

    order = [
        "enter",
        "spec", "lows_a", "cols_even", "cols_low_even", "cols_odd", "cols_low_odd", "rows_even", "rows_odd", "lows_b",
        "fine_rows", "fine_cols", "fine_cols_low", "coarse_cols", "coarse_rows", "coarse_rows_low",
        "rows_back_even", "rows_back_odd", "cols_back_even", "cols_back_odd", "leave", "last", "last_low",
    ]
    places, start = {}, 0
    for name in order:
        places[name] = (start, parts[name].shape[0])
        start += parts[name].shape[0]
    return np.concatenate([parts[name] for name in order], axis=0), places


TABLE, PLACES = build_tables()
CUTS = (0, PLACES["spec"][0], PLACES["fine_rows"][0], TABLE.shape[0])


def dot(left, right):
    return jnp.dot(left, right, preferred_element_type=jnp.float32)


def cut(value):
    high = value.astype(jnp.bfloat16)
    low = (value - high.astype(jnp.float32)).astype(jnp.bfloat16)
    return high, low


def lanes(shape):
    return lax.broadcasted_iota(jnp.int32, shape, 1)


def enter(value, table):
    high, low = cut(value)
    both = dot(high, table)
    return both[:, :128] + both[:, 128:] + dot(low, table[:, :128])


def pack(first, second):
    return jnp.where(lanes(first.shape) < 64, first, second)


def spectrum(gathered, table, low_table, roll):
    high, low = cut(gathered)
    out = dot(table, jnp.concatenate([high, low], axis=0)) + dot(low_table, high)
    both = pack(out[:128], out[128:])
    both = both + roll(both, 64, 1)
    turned = roll(both, 32, 1)
    quarter = lanes((BAND, 128)) >> 5
    outer = (quarter == 0) | (quarter == 3)
    even = jnp.where(outer, both[:BAND], turned[:BAND])
    odd = jnp.where(outer, turned[BAND:], both[BAND:])
    return jnp.where(quarter == 3, -even, even) + jnp.where(quarter == 0, -odd, odd)


def pupil_of(row_shift, col_shift):
    shape = (BAND, 128)
    row = lax.broadcasted_iota(jnp.int32, shape, 0) - BAND // 2 + row_shift
    slot = lanes(shape) & 63
    col = jnp.where(slot < HALF, slot, HALF - slot) + col_shift
    inside = (row * row + col * col <= RAD * RAD) & (slot != HALF)
    return inside.astype(jnp.float32)


def swap(first, second):
    return pack(first, second), pack(second, first)


def coarse_fields(spec, pupils, cols, rows):
    high, low = cut(spec)
    mids = []
    for which in range(2):
        band_high = jnp.concatenate([high * pupil for pupil in pupils[which::2]], axis=0)
        band_low = jnp.concatenate([low * pupil for pupil in pupils[which::2]], axis=0)
        table, low_table = cols[which]
        mids.append(
            dot(jnp.concatenate([band_high, band_low], axis=1), table) + dot(band_high, low_table)
        )
    fields = []
    for group in range(2):
        stacks = ([], [])
        for pair in (2 * group, 2 * group + 1):
            at = slice(BAND * pair, BAND * pair + BAND)
            real = swap(mids[0][at, :128], mids[1][at, :128])
            imag = swap(mids[0][at, 128:], mids[1][at, 128:])
            for parity in range(2):
                stacks[parity].append(jnp.concatenate([real[parity], imag[parity]], axis=0))
        both = []
        for parity in range(2):
            upper, lower = cut(jnp.concatenate(stacks[parity], axis=1))
            table, low_table = rows[parity]
            both.append(dot(table, jnp.concatenate([upper, lower], axis=0)) + dot(low_table, upper))
        fields.append(both)
    return fields


def power_of(field):
    half = ROWS_C // 2
    return field[:half] * field[:half] + field[half:] * field[half:]


def join_image(even, odd, roll):
    return pack(even + roll(even, 64, 1), odd + roll(odd, 64, 1))


def pixels_of(coarse, fine_rows, fine_cols, fine_cols_low):
    first = lanes(coarse.shape) < 64
    coarse = jnp.concatenate([jnp.where(first, coarse, 0.0), jnp.where(first, 0.0, coarse)], axis=0)
    high, low = cut(coarse)
    mid = dot(jnp.concatenate([high, low], axis=1), fine_cols) + dot(high, fine_cols_low)
    return dot(fine_rows, three(mid))


def three(value):
    high, low = cut(value)
    pad = jnp.zeros((TILE - 3 * value.shape[0], value.shape[1]), jnp.bfloat16)
    return jnp.concatenate([high, low, high, pad], axis=0)


def coarse_of(slope, coarse_rows, coarse_rows_low, coarse_cols):
    high, low = cut(slope)
    mid = dot(coarse_rows, high) + dot(coarse_rows, low) + dot(coarse_rows_low, high)
    high, low = cut(mid)
    both = dot(high, coarse_cols)
    return both[:, :128] + both[:, 128:] + dot(low, coarse_cols[:, :128])


def twice(coarse, roll):
    half = ROWS_C // 2
    even, odd = coarse[:half], coarse[half:]
    return pack(even, roll(even, 64, 1)), pack(roll(odd, 64, 1), odd)


def band_grad(total, adjoints, pupils, rows_back, cols_back):
    sides = ([], [])
    for group in range(2):
        even, odd = [dot(rows_back[parity], three(adjoints[group][parity])) for parity in range(2)]
        for pair in range(2):
            at = slice(128 * pair, 128 * pair + 128)
            real = swap(even[:BAND, at], odd[:BAND, at])
            imag = swap(even[BAND:, at], odd[BAND:, at])
            for which in range(2):
                sides[which].append(jnp.concatenate([real[which], imag[which]], axis=1))
    for which in range(2):
        high, low = cut(jnp.concatenate(sides[which], axis=0))
        both = dot(high, cols_back[which])
        term = both[:, :128] + both[:, 128:] + dot(low, cols_back[which][:, :128])
        for k in range(PER_DEV // 2):
            total = total + term[BAND * k : BAND * k + BAND] * pupils[2 * k + which]
    return total


def fold(grad, roll):
    r32, r64, r96 = roll(grad, 32, 1), roll(grad, 64, 1), roll(grad, 96, 1)
    quarter = lanes(grad.shape) >> 5
    upper = jnp.where(
        quarter == 0, grad + r96, jnp.where(quarter == 1, r96 - r64, jnp.where(quarter == 2, r64 + r32, r32 - grad))
    )
    lower = jnp.where(
        quarter == 0, r64 + r32, jnp.where(quarter == 1, grad - r32, jnp.where(quarter == 2, grad + r96, r64 - r96))
    )
    return jnp.concatenate([upper, lower], axis=0)


def row_grads(grad, leave, leave_low, roll):
    high, low = cut(fold(grad, roll))
    out = dot(leave, jnp.concatenate([high, low], axis=0)) + dot(leave_low, high)
    half = out.shape[0] // 2
    return pack(out[:half], out[half:])


def last_step(total, last, last_low):
    first = lanes(total.shape) < 64
    value = jnp.concatenate([jnp.where(first, total, 0.0), jnp.where(first, 0.0, total)], axis=0)
    high, low = cut(value)
    return dot(high, last) + dot(low, last) + dot(high, last_low)


def rank_of(side, along):
    step = jnp.where(along <= DEPTH // 2, 2 * along - 1, 2 * (DEPTH - along))
    return 2 * jnp.maximum(step, 0) + side


def src_of(rank):
    step, side = rank // 2, rank % 2
    half = (step + 1) // 2
    return side * DEPTH + jnp.where(step % 2 == 1, half, (DEPTH - half) % DEPTH)


def repeat(first, last, body):
    def step(k, carry):
        body(k)
        return carry

    lax.fori_loop(first, last, step, 0)


def everything(mask, target, shifts, weights, table, resist, mask_grad, source_grad, *scratch):
    (
        mask_v, target_v, shifts_v, weights_v, table_v,
        left_v, right_v, spec_v, pupil_v, scale_v, image_v, term_v, field_v, power_v,
        printed_v, grad_v, part_v, sums_v, local_sem, send_sem, recv_sem, sums_sem, ready_sem,
    ) = scratch
    tile, src = lax.axis_index("tile"), lax.axis_index("src")
    n_tile = lax.axis_size("tile")
    left, right = tile - 1, tile + 1
    has_left, has_right = tile > 0, tile < n_tile - 1
    side, along = src // DEPTH, src % DEPTH
    rank = rank_of(side, along)
    quad = along // QUAD
    partners = [
        (side + across) % 2 * DEPTH + (along + step) % DEPTH for across, step in ((0, QUAD), (1, 0), (1, QUAD))
    ]
    members = [side * DEPTH + quad * QUAD + (along + k) % QUAD for k in range(1, QUAD)]
    layer = tile // GROUP
    layer_first, layer_last = layer * GROUP, layer * GROUP + GROUP

    def get(name, start=None, stop=None):
        at, size = PLACES[name]
        if start is None:
            return table_v[at : at + size, :]
        return table_v[at : at + size, start:stop]

    def signal(sem, device):
        pl.semaphore_signal(sem, inc=1, device_id=device, device_id_type=MESH)

    def send(source, target_ref, number, device):
        copy = pltpu.make_async_remote_copy(
            src_ref=source,
            dst_ref=target_ref,
            send_sem=send_sem.at[number],
            recv_sem=recv_sem.at[number],
            device_id=device,
            device_id_type=MESH,
        )
        copy.start()

    def wait(ref, sem):
        pltpu.make_async_copy(ref, ref, sem).wait()

    barrier = pltpu.get_barrier_semaphore()

    @pl.when(has_left)
    def _():
        signal(barrier, {"tile": left})

    @pl.when(has_right)
    def _():
        signal(barrier, {"tile": right})

    repeat(rank + 1, N_SRC, lambda k: signal(barrier, {"src": src_of(k)}))
    local = [
        pltpu.make_async_copy(mask, mask_v, local_sem.at[0]),
        pltpu.make_async_copy(shifts, shifts_v, local_sem.at[1]),
        pltpu.make_async_copy(weights, weights_v, local_sem.at[2]),
    ]
    for k in range(3):
        rows = pl.ds(CUTS[k], CUTS[k + 1] - CUTS[k])
        local.append(pltpu.make_async_copy(table.at[rows], table_v.at[rows], local_sem.at[3 + k]))
    local.append(pltpu.make_async_copy(target, target_v, local_sem.at[6]))
    for copy in local:
        copy.start()
    repeat(layer_first, tile, lambda k: signal(barrier, {"tile": k}))
    repeat(tile + 1, n_tile, lambda k: signal(barrier, {"tile": k}))

    ends = has_left.astype(jnp.int32) + has_right.astype(jnp.int32)
    pl.semaphore_wait(barrier, rank + ends + layer_last - 1)

    @pl.when(has_right)
    def _():
        send(mask.at[:, pl.ds(128, 128)], left_v, 0, {"tile": right})

    @pl.when(has_left)
    def _():
        send(mask.at[:, pl.ds(0, 128)], right_v, 1, {"tile": left})

    repeat(0, rank, lambda k: signal(ready_sem.at[rank], {"src": src_of(k)}))

    @pl.when(jnp.logical_not(has_left))
    def _():
        left_v[...] = jnp.zeros_like(left_v)

    @pl.when(jnp.logical_not(has_right))
    def _():
        right_v[...] = jnp.zeros_like(right_v)

    local[1].wait()
    local[2].wait()
    spec_v[src, 8:16, :] = jnp.zeros((8, 128), jnp.float32)
    spec_v[src, 8:10, 0:PER_DEV] = shifts_v[...].astype(jnp.float32)
    spec_v[src, 10:11, 0:PER_DEV] = weights_v[...]
    local[0].wait()
    local[3].wait()
    at = PLACES["enter"][0]
    own = enter(mask_v[...], table_v[at : at + TILE, :])

    @pl.when(has_left)
    def _():
        wait(left_v, recv_sem.at[0])

    @pl.when(has_right)
    def _():
        wait(right_v, recv_sem.at[1])

    margins = jnp.concatenate([left_v[...], right_v[...]], axis=1)
    own = own + enter(margins, table_v[at + TILE : at + 2 * TILE, :])
    spec_v[src, 0:8, :] = pack(own[:8], own[8:])
    piece = pl.ds(0, 11)

    def send_piece(k):
        send(spec_v.at[src, piece], spec_v.at[src, piece], 2, {"src": src_of(k)})

    def answer_piece(k):
        pl.semaphore_wait(ready_sem.at[k], 1)
        send_piece(k)

    repeat(0, rank, send_piece)
    repeat(rank + 1, N_SRC, answer_piece)
    local[4].wait()
    wait(spec_v.at[pl.ds(0, N_SRC - 1), piece], recv_sem.at[2])

    gathered = spec_v[:, 0:8, :].reshape(128, 128)
    spec = spectrum(gathered, get("spec"), get("lows_a", 0, 128), pltpu.roll)
    at = PLACES["lows_b"][0]
    cols = [(get("cols_" + name), get("cols_low_" + name)) for name in ("even", "odd")]
    rows = [
        (get("rows_even"), table_v[at : at + ROWS_C, 128:256]),
        (get("rows_odd"), table_v[at + ROWS_C : at + 2 * ROWS_C, 128:256]),
    ]

    def add_fields(part, images):
        owner = src
        for k, peer in enumerate(partners):
            owner = jnp.where(part == k + 1, peer, owner)
        extra = spec_v[owner, 8:16, :]
        shift = extra[0:2, :].astype(jnp.int32)
        for s in range(PER_DEV):
            pupil_v[part, s] = pupil_of(shift[0:1, s : s + 1], shift[1:2, s : s + 1])
        for pair in range(PER_DEV // 2):
            first, second = [
                jnp.broadcast_to(extra[2:3, s : s + 1], (8, 128)) for s in (2 * pair, 2 * pair + 1)
            ]
            at = slice(128 * (pair % 2), 128 * (pair % 2) + 128)
            for parity, scale in enumerate(swap(first, second)):
                scale_v[part, pair // 2, parity, :, at] = scale
        fields = coarse_fields(
            spec, [pupil_v[part, s].astype(jnp.bfloat16) for s in range(PER_DEV)], cols, rows
        )
        images = list(images)
        for group in range(2):
            for parity in range(2):
                field_v[part, group, parity] = fields[group][parity]
                power = power_of(fields[group][parity])
                power_v[part, group, parity] = power
                power = power * scale_v[part, group, parity, 0:1, :]
                images[parity] = images[parity] + power[:, :128] + power[:, 128:]
        return tuple(images)

    none = jnp.zeros((ROWS_C // 2, 128), jnp.float32)
    image_v[...] = join_image(*lax.fori_loop(0, QUAD, add_fields, (none, none)), pltpu.roll)
    for k, peer in enumerate(members):
        send(image_v, term_v.at[k], 3, {"src": peer})
    local[5].wait()
    local[6].wait()
    wait(term_v, recv_sem.at[3])

    image = pixels_of(
        image_v[...] + term_v[0] + term_v[1] + term_v[2],
        get("fine_rows"),
        get("fine_cols"),
        get("fine_cols_low"),
    )
    printed = jax.nn.sigmoid(STEEP * (image * (1.0 / SOURCES) - THRESH))
    printed_v[...] = printed
    resist[...] = printed_v[pl.ds(pl.multiple_of(src * ROWS, ROWS), ROWS), :]
    goal = target_v[...].astype(jnp.float32)
    slope = (LOSS_SCALE * 2.0 * STEEP) * (printed - goal) * printed * (1.0 - printed)
    coarse = coarse_of(slope, get("coarse_rows"), get("coarse_rows_low"), get("coarse_cols"))

    slopes = twice(coarse, pltpu.roll)
    sums = []
    for pair in range(PER_DEV // 2):
        at = slice(128 * (pair % 2), 128 * (pair % 2) + 128)
        terms = [
            jnp.sum(slopes[parity] * power_v[0, pair // 2, parity, :, at], axis=0, keepdims=True) for parity in range(2)
        ]
        sums.extend(swap(*terms))
    sums = jnp.sum(jnp.concatenate(sums, axis=0), axis=1, keepdims=True)
    spot = (PER_DEV, 128)
    sums = jnp.where(lanes(spot) == lax.broadcasted_iota(jnp.int32, spot, 0), sums, 0.0)
    sums_v[tile] = jnp.sum(sums, axis=0, keepdims=True)

    def send_sums(k):
        pltpu.make_async_remote_copy(
            src_ref=sums_v.at[tile],
            dst_ref=sums_v.at[tile],
            send_sem=send_sem.at[5],
            recv_sem=sums_sem.at[layer],
            device_id={"tile": k},
            device_id_type=MESH,
        ).start()

    repeat(0, tile, send_sums)
    repeat(tile + 1, layer_last, send_sums)

    wide = [jnp.concatenate([slope, slope], axis=1) * (2.0 / SOURCES) for slope in slopes]
    rows_back = [get("rows_back_even"), get("rows_back_odd")]
    cols_back = [get("cols_back_even"), get("cols_back_odd")]

    def add_part(part, total):
        adjoints = []
        for group in range(2):
            adjoints.append([])
            for parity in range(2):
                scaled = wide[parity] * scale_v[part, group, parity, 0:1, :]
                adjoints[group].append(field_v[part, group, parity] * jnp.concatenate([scaled, scaled], axis=0))
        return band_grad(total, adjoints, [pupil_v[part, s] for s in range(PER_DEV)], rows_back, cols_back)

    grad = lax.fori_loop(0, QUAD, add_part, jnp.zeros((BAND, 128), jnp.float32))
    first = PLACES["leave"][0] + 8 * QUAD * (src // QUAD)
    low_first = PLACES["lows_b"][0] + 8 * QUAD * (src // QUAD)

    def halves_of(start, stop, begin):
        begin = pl.multiple_of(begin, 32)
        then = pl.multiple_of(begin + 128, 32)
        return jnp.concatenate(
            [table_v[pl.ds(begin, 8 * QUAD), start:stop], table_v[pl.ds(then, 8 * QUAD), start:stop]], axis=0
        )

    rows = row_grads(grad, halves_of(0, 256, first), halves_of(0, 128, low_first), pltpu.roll)
    grad_v[...] = rows.reshape(QUAD, 8, 128)
    for k, peer in enumerate(members):
        send(grad_v.at[peer % QUAD], part_v.at[k], 4, {"src": peer})

    def finish():
        wait(part_v, recv_sem.at[4])
        total = grad_v[along % QUAD] + part_v[0] + part_v[1] + part_v[2]
        mask_grad[...] = last_step(total, get("last"), get("last_low"))

    def answer_sums(k):
        wait(sums_v.at[pl.ds(k * GROUP, GROUP)], sums_sem.at[k])
        repeat(k * GROUP, k * GROUP + GROUP, send_sums)

    pl.when(layer == 0)(finish)
    repeat(layer + 1, n_tile // GROUP, answer_sums)
    pl.when(layer > 0)(finish)
    wait(sums_v.at[pl.ds(0, GROUP - 1)], sums_sem.at[layer])
    repeat(0, layer, lambda k: wait(sums_v.at[pl.ds(k * GROUP, GROUP)], sums_sem.at[k]))
    source_grad[...] = jnp.sum(sums_v[...], axis=0) * (1.0 / (SOURCES * n_tile * TILE * TILE))

    @pl.when(has_right)
    def _():
        wait(left_v, send_sem.at[0])

    @pl.when(has_left)
    def _():
        wait(right_v, send_sem.at[1])

    wait(spec_v.at[pl.ds(0, N_SRC - 1), piece], send_sem.at[2])
    wait(term_v, send_sem.at[3])
    wait(part_v, send_sem.at[4])
    wait(sums_v.at[pl.ds(0, n_tile - 1)], send_sem.at[5])


def hand_over(resist, mask_grad, source_grad, resist_out, mask_grad_out, source_grad_out, sem):
    copies = [
        pltpu.make_async_copy(resist, resist_out, sem.at[0]),
        pltpu.make_async_copy(mask_grad, mask_grad_out, sem.at[1]),
    ]
    for copy in copies:
        copy.start()
    source_grad_out[...] = source_grad[0, :PER_DEV]
    for copy in copies:
        copy.wait()


def local(mask, target, shifts, weights):
    f32 = jnp.float32
    anywhere = pl.BlockSpec(memory_space=pl.ANY)
    inside = pl.BlockSpec(memory_space=pltpu.VMEM)
    results = pl.pallas_call(
        everything,
        out_shape=(
            pltpu.VMEM((ROWS, TILE), f32),
            pltpu.VMEM((ROWS, TILE), f32),
            pltpu.VMEM((1, 128), f32),
        ),
        in_specs=[anywhere] * 5,
        out_specs=(inside, inside, inside),
        scratch_shapes=[
            pltpu.VMEM((ROWS, TILE), f32),
            pltpu.VMEM((TILE, TILE), jnp.int32),
            pltpu.VMEM((2, PER_DEV), jnp.int32),
            pltpu.VMEM((1, PER_DEV), f32),
            pltpu.VMEM(TABLE.shape, jnp.bfloat16),
            pltpu.VMEM((ROWS, 128), f32),
            pltpu.VMEM((ROWS, 128), f32),
            pltpu.VMEM((N_SRC, 16, 128), f32),
            pltpu.VMEM((QUAD, PER_DEV, BAND, 128), f32),
            pltpu.VMEM((QUAD, 2, 2, 8, 256), f32),
            pltpu.VMEM((ROWS_C // 2, 128), f32),
            pltpu.VMEM((QUAD - 1, ROWS_C // 2, 128), f32),
            pltpu.VMEM((QUAD, 2, 2, ROWS_C, 256), f32),
            pltpu.VMEM((QUAD, 2, 2, ROWS_C // 2, 256), f32),
            pltpu.VMEM((TILE, TILE), f32),
            pltpu.VMEM((QUAD, 8, 128), f32),
            pltpu.VMEM((QUAD - 1, 8, 128), f32),
            pltpu.VMEM((N_TILE, 1, 128), f32),
            pltpu.SemaphoreType.DMA((7,)),
            pltpu.SemaphoreType.DMA((6,)),
            pltpu.SemaphoreType.DMA((5,)),
            pltpu.SemaphoreType.DMA((DEPTH,)),
            pltpu.SemaphoreType.REGULAR((N_SRC,)),
        ],
        compiler_params=pltpu.CompilerParams(
            collective_id=0, has_side_effects=True, vmem_limit_bytes=60 * 1024 * 1024
        ),
    )(mask, target, shifts.T, weights.reshape(1, PER_DEV), jnp.asarray(TABLE))
    return pl.pallas_call(
        hand_over,
        out_shape=(
            jax.ShapeDtypeStruct((ROWS, TILE), f32),
            jax.ShapeDtypeStruct((ROWS, TILE), f32),
            jax.ShapeDtypeStruct((PER_DEV,), f32),
        ),
        in_specs=[inside] * 3,
        out_specs=(anywhere, anywhere, inside),
        scratch_shapes=[pltpu.SemaphoreType.DMA((2,))],
    )(*[pltpu.with_memory_space_constraint(result, pltpu.VMEM) for result in results])


def solution(mesh):
    placed = (P("src", "tile"), P(None, "tile"), P("src", None), P("src"))
    return jax.shard_map(
        local,
        mesh=mesh,
        in_specs=placed,
        out_specs=(P("src", "tile"), P("src", "tile"), P("src")),
        check_vma=False,
    )
```

time: 394 us -> 40.4 us (0.10)
  the two profiles are of different devices: /device:TPU:4 before, /device:TPU:1 now
where the time goes in v1:
time: 40.4 us; the launch traced here: 40.2 us
  Pallas kernels  39.6 us (98%)
  between operations  0.64 us (2%)
    pallas_call x1, Pallas kernels, local(): pl.pallas_call(everything, out_shape=(pltpu.VMEM((ROWS, TILE), f32), pltp...  38.4 us
    pallas_call x1, Pallas kernels, local(): pl.pallas_call(hand_over, out_shape=(jax.ShapeDtypeStruct((ROWS, TILE), f...  1.14 us

profile of v1, /device:TPU:1, one launch (start us, length us, event | category | flops | bytes accessed | tf_op | source)
XLA Modules:
  0.0 40.2 jit_solution(12580808406526711529)
XLA Ops:
  0.6 38.4 %shard_map.76 = (f32[16,256]{1,0:T(8,128)S(1)}, f32[16,256]{1,0:T(8,128)S(1)}, f32[1,128]{1,0:T(1,128)S(1)}) custom-call(f32[16,256]{1,0:T(8,128)} %mask.1, s32[256,256]{1,0:T(8,128)} %target.1, s32[2,8]{1,0:T(2,128)} %bitcast.2, f32[1,8]{1,0:T(1,128)} %bitcast.3, bf16[4544,256]{1,0:T(8,128)(2,1)} %constant.2.clone.table), custom_call_target="tpu_custom_call" | custom-call | tf_op jit(solution)/shard_map/pallas_call | solution.py:617
  39.1 1.1 %shard_map.77 = (f32[16,256]{1,0:T(8,128)}, f32[16,256]{1,0:T(8,128)}, f32[8]{0:T(128)}) custom-call(f32[16,256]{1,0:T(8,128)S(1)} %get-tuple-element.6.resist, f32[16,256]{1,0:T(8,128)S(1)} %get-tuple-element.7.mask_grad, f32[1,128]{1,0:T(1,128)S(1)} %get-tuple-element.8.source_grad), custom_call_target="tpu_custom_call" | custom-call | tf_op jit(solution)/shard_map/pallas_call | solution.py:655

commit v2 on v1

--- a/solution.py
+++ b/solution.py
@@ -29,6 +29,7 @@
 QUAD = 4
 GROUP = 4
 DEPTH = 8
+HUB = 2 * GROUP
 
 MESH = pl.DeviceIdType.MESH
 BF16 = ml_dtypes.bfloat16
@@ -335,7 +336,7 @@
     (
         mask_v, target_v, shifts_v, weights_v, table_v,
         left_v, right_v, spec_v, pupil_v, scale_v, image_v, term_v, field_v, power_v,
-        printed_v, grad_v, part_v, sums_v, local_sem, send_sem, recv_sem, sums_sem, ready_sem,
+        printed_v, grad_v, part_v, sums_v, total_v, local_sem, send_sem, recv_sem, ready_sem, hub_sem,
     ) = scratch
     tile, src = lax.axis_index("tile"), lax.axis_index("src")
     n_tile = lax.axis_size("tile")
@@ -349,7 +350,8 @@
     ]
     members = [side * DEPTH + quad * QUAD + (along + k) % QUAD for k in range(1, QUAD)]
     layer = tile // GROUP
-    layer_first, layer_last = layer * GROUP, layer * GROUP + GROUP
+    place = tile % GROUP
+    is_hub, is_teller = tile < HUB, layer == 1
 
     def get(name, start=None, stop=None):
         at, size = PLACES[name]
@@ -396,11 +398,10 @@
     local.append(pltpu.make_async_copy(target, target_v, local_sem.at[6]))
     for copy in local:
         copy.start()
-    repeat(layer_first, tile, lambda k: signal(barrier, {"tile": k}))
-    repeat(tile + 1, n_tile, lambda k: signal(barrier, {"tile": k}))
+    repeat(jnp.where(is_hub, tile + 1, n_tile), n_tile, lambda k: signal(barrier, {"tile": k}))
 
     ends = has_left.astype(jnp.int32) + has_right.astype(jnp.int32)
-    pl.semaphore_wait(barrier, rank + ends + layer_last - 1)
+    pl.semaphore_wait(barrier, rank + ends + jnp.minimum(tile, HUB))
 
     @pl.when(has_right)
     def _():
@@ -452,6 +453,12 @@
 
     repeat(0, rank, send_piece)
     repeat(rank + 1, N_SRC, answer_piece)
+    repeat(0, jnp.where(is_hub, tile, 0), lambda k: signal(hub_sem.at[0], {"tile": k}))
+
+    @pl.when(jnp.logical_not(is_hub))
+    def _():
+        signal(hub_sem.at[1], {"tile": GROUP + place})
+
     local[4].wait()
     wait(spec_v.at[pl.ds(0, N_SRC - 1), piece], recv_sem.at[2])
 
@@ -531,13 +538,12 @@
             src_ref=sums_v.at[tile],
             dst_ref=sums_v.at[tile],
             send_sem=send_sem.at[5],
-            recv_sem=sums_sem.at[layer],
+            recv_sem=recv_sem.at[5],
             device_id={"tile": k},
             device_id_type=MESH,
         ).start()
 
-    repeat(0, tile, send_sums)
-    repeat(tile + 1, layer_last, send_sums)
+    repeat(0, jnp.minimum(tile, HUB), send_sums)
 
     wide = [jnp.concatenate([slope, slope], axis=1) * (2.0 / SOURCES) for slope in slopes]
     rows_back = [get("rows_back_even"), get("rows_back_odd")]
@@ -568,21 +574,47 @@
     for k, peer in enumerate(members):
         send(grad_v.at[peer % QUAD], part_v.at[k], 4, {"src": peer})
 
-    def finish():
-        wait(part_v, recv_sem.at[4])
-        total = grad_v[along % QUAD] + part_v[0] + part_v[1] + part_v[2]
-        mask_grad[...] = last_step(total, get("last"), get("last_low"))
-
-    def answer_sums(k):
-        wait(sums_v.at[pl.ds(k * GROUP, GROUP)], sums_sem.at[k])
-        repeat(k * GROUP, k * GROUP + GROUP, send_sums)
-
-    pl.when(layer == 0)(finish)
-    repeat(layer + 1, n_tile // GROUP, answer_sums)
-    pl.when(layer > 0)(finish)
-    wait(sums_v.at[pl.ds(0, GROUP - 1)], sums_sem.at[layer])
-    repeat(0, layer, lambda k: wait(sums_v.at[pl.ds(k * GROUP, GROUP)], sums_sem.at[k]))
-    source_grad[...] = jnp.sum(sums_v[...], axis=0) * (1.0 / (SOURCES * n_tile * TILE * TILE))
+
+    @pl.when(tile < HUB - 1)
+    def _():
+        pl.semaphore_wait(hub_sem.at[0], HUB - 1 - tile)
+        repeat(tile + 1, HUB, send_sums)
+
+    wait(part_v, recv_sem.at[4])
+    total = grad_v[along % QUAD] + part_v[0] + part_v[1] + part_v[2]
+    mask_grad[...] = last_step(total, get("last"), get("last_low"))
+
+    @pl.when(is_hub)
+    def _():
+        wait(sums_v.at[pl.ds(0, n_tile - 1)], recv_sem.at[5])
+        total_v[...] = jnp.sum(sums_v[...], axis=0) * (1.0 / (SOURCES * n_tile * TILE * TILE))
+
+    def tell(k):
+        send(total_v, total_v, 6, {"tile": k * GROUP + place})
+
+    @pl.when(is_teller)
+    def _():
+        pl.semaphore_wait(hub_sem.at[1], n_tile // GROUP - 2)
+        repeat(2, n_tile // GROUP, tell)
+
+    @pl.when(jnp.logical_not(is_hub))
+    def _():
+        wait(total_v, recv_sem.at[6])
+
+    source_grad[...] = total_v[...]
+
+    @pl.when(is_teller)
+    def _():
+        wait(sums_v.at[pl.ds(0, n_tile // GROUP - 2)], send_sem.at[6])
+
+    @pl.when(is_hub)
+    def _():
+        wait(sums_v.at[pl.ds(0, HUB - 1)], send_sem.at[5])
+
+    @pl.when(jnp.logical_not(is_hub))
+    def _():
+        wait(sums_v.at[pl.ds(0, HUB)], send_sem.at[5])
+
 
     @pl.when(has_right)
     def _():
@@ -595,7 +627,6 @@
     wait(spec_v.at[pl.ds(0, N_SRC - 1), piece], send_sem.at[2])
     wait(term_v, send_sem.at[3])
     wait(part_v, send_sem.at[4])
-    wait(sums_v.at[pl.ds(0, n_tile - 1)], send_sem.at[5])
 
 
 def hand_over(resist, mask_grad, source_grad, resist_out, mask_grad_out, source_grad_out, sem):
@@ -642,11 +673,12 @@
             pltpu.VMEM((QUAD, 8, 128), f32),
             pltpu.VMEM((QUAD - 1, 8, 128), f32),
             pltpu.VMEM((N_TILE, 1, 128), f32),
+            pltpu.VMEM((1, 128), f32),
             pltpu.SemaphoreType.DMA((7,)),
-            pltpu.SemaphoreType.DMA((6,)),
-            pltpu.SemaphoreType.DMA((5,)),
-            pltpu.SemaphoreType.DMA((DEPTH,)),
+            pltpu.SemaphoreType.DMA((7,)),
+            pltpu.SemaphoreType.DMA((7,)),
             pltpu.SemaphoreType.REGULAR((N_SRC,)),
+            pltpu.SemaphoreType.REGULAR((2,)),
         ],
         compiler_params=pltpu.CompilerParams(
             collective_id=0, has_side_effects=True, vmem_limit_bytes=60 * 1024 * 1024

time: 40.4 us -> 39.6 us (0.980)
  Pallas kernels: 39.6 us -> 38.7 us
    pallas_call x1, Pallas kernels: 38.4 us -> 37.6 us  [local(): pl.pallas_call(everything, out_shape=(pltpu.VMEM((ROWS, TILE), f32), pltp...]
where the time goes in v2:
time: 39.6 us; the launch traced here: 39.4 us
  Pallas kernels  38.7 us (98%)
  between operations  0.64 us (2%)
    pallas_call x1, Pallas kernels, local(): pl.pallas_call(everything, out_shape=(pltpu.VMEM((ROWS, TILE), f32), pltp...  37.6 us
    pallas_call x1, Pallas kernels, local(): pl.pallas_call(hand_over, out_shape=(jax.ShapeDtypeStruct((ROWS, TILE), f...  1.14 us

profile of v2, /device:TPU:1, one launch (start us, length us, event | category | flops | bytes accessed | tf_op | source)
XLA Modules:
  0.0 39.4 jit_solution(14774709202674965743)
XLA Ops:
  0.6 37.6 %shard_map.76 = (f32[16,256]{1,0:T(8,128)S(1)}, f32[16,256]{1,0:T(8,128)S(1)}, f32[1,128]{1,0:T(1,128)S(1)}) custom-call(f32[16,256]{1,0:T(8,128)} %mask.1, s32[256,256]{1,0:T(8,128)} %target.1, s32[2,8]{1,0:T(2,128)} %bitcast.2, f32[1,8]{1,0:T(1,128)} %bitcast.3, bf16[4544,256]{1,0:T(8,128)(2,1)} %constant.2.clone.table), custom_call_target="tpu_custom_call" | custom-call | tf_op jit(solution)/shard_map/pallas_call | solution.py:648
  38.2 1.1 %shard_map.77 = (f32[16,256]{1,0:T(8,128)}, f32[16,256]{1,0:T(8,128)}, f32[8]{0:T(128)}) custom-call(f32[16,256]{1,0:T(8,128)S(1)} %get-tuple-element.6.resist, f32[16,256]{1,0:T(8,128)S(1)} %get-tuple-element.7.mask_grad, f32[1,128]{1,0:T(1,128)S(1)} %get-tuple-element.8.source_grad), custom_call_target="tpu_custom_call" | custom-call | tf_op jit(solution)/shard_map/pallas_call | solution.py:687

commit v3 on v2

--- a/solution.py
+++ b/solution.py
@@ -500,7 +500,7 @@
         return tuple(images)
 
     none = jnp.zeros((ROWS_C // 2, 128), jnp.float32)
-    image_v[...] = join_image(*lax.fori_loop(0, QUAD, add_fields, (none, none)), pltpu.roll)
+    image_v[...] = join_image(*lax.fori_loop(0, QUAD, add_fields, (none, none), unroll=True), pltpu.roll)
     for k, peer in enumerate(members):
         send(image_v, term_v.at[k], 3, {"src": peer})
     local[5].wait()

time: 39.6 us -> 38.8 us (0.980)
  Pallas kernels: 38.7 us -> 38 us
    pallas_call x1, Pallas kernels: 37.6 us -> 36.8 us  [local(): pl.pallas_call(everything, out_shape=(pltpu.VMEM((ROWS, TILE), f32), pltp...]
where the time goes in v3:
time: 38.8 us; the launch traced here: 38.6 us
  Pallas kernels  38 us (98%)
  between operations  0.64 us (2%)
    pallas_call x1, Pallas kernels, local(): pl.pallas_call(everything, out_shape=(pltpu.VMEM((ROWS, TILE), f32), pltp...  36.8 us
    pallas_call x1, Pallas kernels, local(): pl.pallas_call(hand_over, out_shape=(jax.ShapeDtypeStruct((ROWS, TILE), f...  1.14 us

profile of v3, /device:TPU:1, one launch (start us, length us, event | category | flops | bytes accessed | tf_op | source)
XLA Modules:
  0.0 38.6 jit_solution(4406506229829616087)
XLA Ops:
  0.6 36.8 %shard_map.76 = (f32[16,256]{1,0:T(8,128)S(1)}, f32[16,256]{1,0:T(8,128)S(1)}, f32[1,128]{1,0:T(1,128)S(1)}) custom-call(f32[16,256]{1,0:T(8,128)} %mask.1, s32[256,256]{1,0:T(8,128)} %target.1, s32[2,8]{1,0:T(2,128)} %bitcast.2, f32[1,8]{1,0:T(1,128)} %bitcast.3, bf16[4544,256]{1,0:T(8,128)(2,1)} %constant.2.clone.table), custom_call_target="tpu_custom_call" | custom-call | tf_op jit(solution)/shard_map/pallas_call | solution.py:648
  37.5 1.1 %shard_map.77 = (f32[16,256]{1,0:T(8,128)}, f32[16,256]{1,0:T(8,128)}, f32[8]{0:T(128)}) custom-call(f32[16,256]{1,0:T(8,128)S(1)} %get-tuple-element.6.resist, f32[16,256]{1,0:T(8,128)S(1)} %get-tuple-element.7.mask_grad, f32[1,128]{1,0:T(1,128)S(1)} %get-tuple-element.8.source_grad), custom_call_target="tpu_custom_call" | custom-call | tf_op jit(solution)/shard_map/pallas_call | solution.py:687

commit v4 on v3

--- a/solution.py
+++ b/solution.py
@@ -24,6 +24,7 @@
 SOURCES = 128
 ROWS = 16
 HALF = 32
+POINTS_R = 66
 ROWS_C = 80
 COLS_C = 128
 QUAD = 4
@@ -56,6 +57,10 @@
     place = np.arange(TILE) + MARGIN
     offset = place[:, None] / EXT - np.arange(points)[None, :] / points
     return np.cos(2.0 * np.pi * order[None, None, :] * offset[:, :, None]).sum(axis=2) / points
+
+
+def padded(rows):
+    return np.concatenate([rows, np.zeros((ROWS_C // 2 - rows.shape[0], rows.shape[1]))], axis=0)
 
 
 def build_tables():
@@ -82,7 +87,7 @@
     parts["spec"] = np.concatenate([high, high], axis=1)
     spec_low = low
 
-    inter_rows, inter_cols = 2.0 * interpolation(ROWS_C), interpolation(COLS_C)
+    inter_rows, inter_cols = 2.0 * interpolation(POINTS_R), interpolation(COLS_C)
     even, odd = np.arange(0, COLS_C, 2), np.arange(1, COLS_C, 2)
     for name, order in (("even", np.concatenate([even, odd])), ("odd", np.concatenate([odd, even]))):
         real, imag = waves(slots, order, COLS_C)
@@ -98,8 +103,8 @@
 
     lows = []
     for name, start in (("even", 0), ("odd", 1)):
-        real, imag = waves(row_freq, np.arange(start, ROWS_C, 2), ROWS_C)
-        real, imag = real.T, imag.T
+        real, imag = waves(row_freq, np.arange(start, POINTS_R, 2), POINTS_R)
+        real, imag = padded(real.T), padded(imag.T)
         high, low = halves(
             np.concatenate(
                 [np.concatenate([real, -imag], axis=1), np.concatenate([imag, real], axis=1)], axis=0
@@ -111,8 +116,8 @@
         parts["rows_back_" + name] = np.concatenate([high.T, high.T, low.T, pad], axis=1)
     rows_low = np.concatenate(lows, axis=0)
 
-    mixed = np.concatenate([np.arange(0, ROWS_C, 2), np.arange(1, ROWS_C, 2)])
-    inter_rows, inter_cols = inter_rows[:, mixed], inter_cols[:, np.concatenate([even, odd])]
+    inter_rows = np.concatenate([padded(inter_rows[:, 0::2].T), padded(inter_rows[:, 1::2].T)], axis=0).T
+    inter_cols = inter_cols[:, np.concatenate([even, odd])]
     high, low = halves(inter_rows)
     pad = np.zeros((TILE, TILE - 3 * ROWS_C), BF16)
     parts["fine_rows"] = np.concatenate([high, high, low, pad], axis=1)
@@ -191,12 +196,11 @@
 
 
 def pupil_of(row_shift, col_shift):
-    shape = (BAND, 128)
-    row = lax.broadcasted_iota(jnp.int32, shape, 0) - BAND // 2 + row_shift
-    slot = lanes(shape) & 63
+    row = lax.broadcasted_iota(jnp.int32, (BAND, 128), 0) - BAND // 2 + row_shift
+    slot = lanes((1, 128)) & 63
     col = jnp.where(slot < HALF, slot, HALF - slot) + col_shift
-    inside = (row * row + col * col <= RAD * RAD) & (slot != HALF)
-    return inside.astype(jnp.float32)
+    room = jnp.where(slot == HALF, -1, RAD * RAD - col * col)
+    return jnp.where(row * row <= room, 1.0, 0.0)
 
 
 def swap(first, second):
@@ -314,14 +318,12 @@
 
 
 def rank_of(side, along):
-    step = jnp.where(along <= DEPTH // 2, 2 * along - 1, 2 * (DEPTH - along))
-    return 2 * jnp.maximum(step, 0) + side
+    return 2 * jnp.where(along < DEPTH // 2, along, DEPTH + DEPTH // 2 - 1 - along) + side
 
 
 def src_of(rank):
     step, side = rank // 2, rank % 2
-    half = (step + 1) // 2
-    return side * DEPTH + jnp.where(step % 2 == 1, half, (DEPTH - half) % DEPTH)
+    return side * DEPTH + jnp.where(step < DEPTH // 2, step, DEPTH + DEPTH // 2 - 1 - step)
 
 
 def repeat(first, last, body):
@@ -396,8 +398,8 @@
         rows = pl.ds(CUTS[k], CUTS[k + 1] - CUTS[k])
         local.append(pltpu.make_async_copy(table.at[rows], table_v.at[rows], local_sem.at[3 + k]))
     local.append(pltpu.make_async_copy(target, target_v, local_sem.at[6]))
-    for copy in local:
-        copy.start()
+    local[0].start()
+    local[3].start()
     repeat(jnp.where(is_hub, tile + 1, n_tile), n_tile, lambda k: signal(barrier, {"tile": k}))
 
     ends = has_left.astype(jnp.int32) + has_right.astype(jnp.int32)
@@ -411,7 +413,10 @@
     def _():
         send(mask.at[:, pl.ds(0, 128)], right_v, 1, {"tile": left})
 
+    for k in (1, 2, 4, 5, 6):
+        local[k].start()
     repeat(0, rank, lambda k: signal(ready_sem.at[rank], {"src": src_of(k)}))
+    term_v[:, POINTS_R // 2 :, :] = jnp.zeros((QUAD - 1, (ROWS_C - POINTS_R) // 2, 128), jnp.float32)
 
     @pl.when(jnp.logical_not(has_left))
     def _():
@@ -451,7 +456,8 @@
         pl.semaphore_wait(ready_sem.at[k], 1)
         send_piece(k)
 
-    repeat(0, rank, send_piece)
+    repeat(0, (rank + 1) // 2, lambda k: send_piece(2 * k))
+    repeat(0, rank // 2, lambda k: send_piece(2 * k + 1))
     repeat(rank + 1, N_SRC, answer_piece)
     repeat(0, jnp.where(is_hub, tile, 0), lambda k: signal(hub_sem.at[0], {"tile": k}))
 
@@ -501,11 +507,12 @@
 
     none = jnp.zeros((ROWS_C // 2, 128), jnp.float32)
     image_v[...] = join_image(*lax.fori_loop(0, QUAD, add_fields, (none, none), unroll=True), pltpu.roll)
+    image_rows = pl.ds(0, POINTS_R // 2)
     for k, peer in enumerate(members):
-        send(image_v, term_v.at[k], 3, {"src": peer})
+        send(image_v.at[image_rows], term_v.at[k, image_rows], 3, {"src": peer})
     local[5].wait()
     local[6].wait()
-    wait(term_v, recv_sem.at[3])
+    wait(term_v.at[:, image_rows], recv_sem.at[3])
 
     image = pixels_of(
         image_v[...] + term_v[0] + term_v[1] + term_v[2],
@@ -625,7 +632,7 @@
         wait(right_v, send_sem.at[1])
 
     wait(spec_v.at[pl.ds(0, N_SRC - 1), piece], send_sem.at[2])
-    wait(term_v, send_sem.at[3])
+    wait(term_v.at[:, image_rows], send_sem.at[3])
     wait(part_v, send_sem.at[4])
 
 

time: 38.8 us -> 36.3 us (0.936)
  Pallas kernels: 38 us -> 35.5 us
    pallas_call x1, Pallas kernels: 36.8 us -> 34.4 us  [local(): pl.pallas_call(everything, out_shape=(pltpu.VMEM((ROWS, TILE), f32), pltp...]
where the time goes in v4:
time: 36.3 us; the launch traced here: 36.2 us
  Pallas kernels  35.5 us (98%)
  between operations  0.64 us (2%)
    pallas_call x1, Pallas kernels, local(): pl.pallas_call(everything, out_shape=(pltpu.VMEM((ROWS, TILE), f32), pltp...  34.4 us
    pallas_call x1, Pallas kernels, local(): pl.pallas_call(hand_over, out_shape=(jax.ShapeDtypeStruct((ROWS, TILE), f...  1.14 us

profile of v4, /device:TPU:1, one launch (start us, length us, event | category | flops | bytes accessed | tf_op | source)
XLA Modules:
  0.0 36.2 jit_solution(3074862288458196248)
XLA Ops:
  0.6 34.4 %shard_map.76 = (f32[16,256]{1,0:T(8,128)S(1)}, f32[16,256]{1,0:T(8,128)S(1)}, f32[1,128]{1,0:T(1,128)S(1)}) custom-call(f32[16,256]{1,0:T(8,128)} %mask.1, s32[256,256]{1,0:T(8,128)} %target.1, s32[2,8]{1,0:T(2,128)} %bitcast.2, f32[1,8]{1,0:T(1,128)} %bitcast.3, bf16[4544,256]{1,0:T(8,128)(2,1)} %constant.2.clone.table), custom_call_target="tpu_custom_call" | custom-call | tf_op jit(solution)/shard_map/pallas_call | solution.py:655
  35.0 1.1 %shard_map.77 = (f32[16,256]{1,0:T(8,128)}, f32[16,256]{1,0:T(8,128)}, f32[8]{0:T(128)}) custom-call(f32[16,256]{1,0:T(8,128)S(1)} %get-tuple-element.6.resist, f32[16,256]{1,0:T(8,128)S(1)} %get-tuple-element.7.mask_grad, f32[1,128]{1,0:T(1,128)S(1)} %get-tuple-element.8.source_grad), custom_call_target="tpu_custom_call" | custom-call | tf_op jit(solution)/shard_map/pallas_call | solution.py:694

commit v5 on v4

--- a/solution.py
+++ b/solution.py
@@ -326,6 +326,10 @@
     return side * DEPTH + jnp.where(step < DEPTH // 2, step, DEPTH + DEPTH // 2 - 1 - step)
 
 
+RANKED = tuple(side * DEPTH + along for along in (0, 1, 2, 3, 7, 6, 5, 4) for side in range(2))
+SERVED = tuple(range(0, N_SRC, 2)) + tuple(range(1, N_SRC, 2))
+
+
 def repeat(first, last, body):
     def step(k, carry):
         body(k)
@@ -337,7 +341,7 @@
 def everything(mask, target, shifts, weights, table, resist, mask_grad, source_grad, *scratch):
     (
         mask_v, target_v, shifts_v, weights_v, table_v,
-        left_v, right_v, spec_v, pupil_v, scale_v, image_v, term_v, field_v, power_v,
+        left_v, right_v, spec_v, pupil_v, scale_v, term_v, field_v, power_v,
         printed_v, grad_v, part_v, sums_v, total_v, local_sem, send_sem, recv_sem, ready_sem, hub_sem,
     ) = scratch
     tile, src = lax.axis_index("tile"), lax.axis_index("src")
@@ -415,8 +419,7 @@
 
     for k in (1, 2, 4, 5, 6):
         local[k].start()
-    repeat(0, rank, lambda k: signal(ready_sem.at[rank], {"src": src_of(k)}))
-    term_v[:, POINTS_R // 2 :, :] = jnp.zeros((QUAD - 1, (ROWS_C - POINTS_R) // 2, 128), jnp.float32)
+    term_v[:, POINTS_R // 2 :, :] = jnp.zeros((QUAD, (ROWS_C - POINTS_R) // 2, 128), jnp.float32)
 
     @pl.when(jnp.logical_not(has_left))
     def _():
@@ -435,6 +438,8 @@
     local[3].wait()
     at = PLACES["enter"][0]
     own = enter(mask_v[...], table_v[at : at + TILE, :])
+    for k in SERVED:
+        pl.when(k < rank)(functools.partial(signal, ready_sem.at[rank], {"src": RANKED[k]}))
 
     @pl.when(has_left)
     def _():
@@ -450,15 +455,16 @@
     piece = pl.ds(0, 11)
 
     def send_piece(k):
-        send(spec_v.at[src, piece], spec_v.at[src, piece], 2, {"src": src_of(k)})
+        send(spec_v.at[src, piece], spec_v.at[src, piece], 2, {"src": RANKED[k]})
 
     def answer_piece(k):
         pl.semaphore_wait(ready_sem.at[k], 1)
         send_piece(k)
 
-    repeat(0, (rank + 1) // 2, lambda k: send_piece(2 * k))
-    repeat(0, rank // 2, lambda k: send_piece(2 * k + 1))
-    repeat(rank + 1, N_SRC, answer_piece)
+    for k in SERVED:
+        pl.when(k < rank)(functools.partial(send_piece, k))
+    for k in range(1, N_SRC):
+        pl.when(k > rank)(functools.partial(answer_piece, k))
     repeat(0, jnp.where(is_hub, tile, 0), lambda k: signal(hub_sem.at[0], {"tile": k}))
 
     @pl.when(jnp.logical_not(is_hub))
@@ -506,16 +512,23 @@
         return tuple(images)
 
     none = jnp.zeros((ROWS_C // 2, 128), jnp.float32)
-    image_v[...] = join_image(*lax.fori_loop(0, QUAD, add_fields, (none, none), unroll=True), pltpu.roll)
+    image = lax.fori_loop(0, QUAD, add_fields, (none, none), unroll=True)
+    place_in_quad = along % QUAD
+    term_v[place_in_quad] = join_image(*image, pltpu.roll)
     image_rows = pl.ds(0, POINTS_R // 2)
-    for k, peer in enumerate(members):
-        send(image_v.at[image_rows], term_v.at[k, image_rows], 3, {"src": peer})
+    mine = term_v.at[place_in_quad, image_rows]
+
+    def send_image(k):
+        send(mine, mine, 3, {"src": side * DEPTH + quad * QUAD + k})
+
+    for k in range(QUAD):
+        pl.when(k != place_in_quad)(functools.partial(send_image, k))
     local[5].wait()
     local[6].wait()
-    wait(term_v.at[:, image_rows], recv_sem.at[3])
+    wait(term_v.at[pl.ds(0, QUAD - 1), image_rows], recv_sem.at[3])
 
     image = pixels_of(
-        image_v[...] + term_v[0] + term_v[1] + term_v[2],
+        term_v[0] + term_v[1] + term_v[2] + term_v[3],
         get("fine_rows"),
         get("fine_cols"),
         get("fine_cols_low"),
@@ -550,7 +563,9 @@
             device_id_type=MESH,
         ).start()
 
-    repeat(0, jnp.minimum(tile, HUB), send_sums)
+    for k in range(HUB):
+        first = k + 1 - 2 * (k % 2)
+        pl.when(first < tile)(functools.partial(send_sums, first))
 
     wide = [jnp.concatenate([slope, slope], axis=1) * (2.0 / SOURCES) for slope in slopes]
     rows_back = [get("rows_back_even"), get("rows_back_odd")]
@@ -632,7 +647,7 @@
         wait(right_v, send_sem.at[1])
 
     wait(spec_v.at[pl.ds(0, N_SRC - 1), piece], send_sem.at[2])
-    wait(term_v.at[:, image_rows], send_sem.at[3])
+    wait(term_v.at[pl.ds(0, QUAD - 1), image_rows], send_sem.at[3])
     wait(part_v, send_sem.at[4])
 
 
@@ -672,8 +687,7 @@
             pltpu.VMEM((N_SRC, 16, 128), f32),
             pltpu.VMEM((QUAD, PER_DEV, BAND, 128), f32),
             pltpu.VMEM((QUAD, 2, 2, 8, 256), f32),
-            pltpu.VMEM((ROWS_C // 2, 128), f32),
-            pltpu.VMEM((QUAD - 1, ROWS_C // 2, 128), f32),
+            pltpu.VMEM((QUAD, ROWS_C // 2, 128), f32),
             pltpu.VMEM((QUAD, 2, 2, ROWS_C, 256), f32),
             pltpu.VMEM((QUAD, 2, 2, ROWS_C // 2, 256), f32),
             pltpu.VMEM((TILE, TILE), f32),

time: 36.3 us -> 37 us (1.019); the launches traced: 36.2 us -> 36.4 us
  no operation moved by 1% of the time
where the time goes in v5:
time: 37 us; the launch traced here: 36.4 us
  Pallas kernels  35.7 us (96%)
  between operations  0.64 us (2%)
    pallas_call x1, Pallas kernels, local(): pl.pallas_call(everything, out_shape=(pltpu.VMEM((ROWS, TILE), f32), pltp...  34.6 us
    pallas_call x1, Pallas kernels, local(): pl.pallas_call(hand_over, out_shape=(jax.ShapeDtypeStruct((ROWS, TILE), f...  1.14 us

profile of v5, /device:TPU:1, one launch (start us, length us, event | category | flops | bytes accessed | tf_op | source)
XLA Modules:
  0.0 36.4 jit_solution(732959869583958888)
XLA Ops:
  0.6 34.6 %shard_map.76 = (f32[16,256]{1,0:T(8,128)S(1)}, f32[16,256]{1,0:T(8,128)S(1)}, f32[1,128]{1,0:T(1,128)S(1)}) custom-call(f32[16,256]{1,0:T(8,128)} %mask.1, s32[256,256]{1,0:T(8,128)} %target.1, s32[2,8]{1,0:T(2,128)} %bitcast.2, f32[1,8]{1,0:T(1,128)} %bitcast.3, bf16[4544,256]{1,0:T(8,128)(2,1)} %constant.2.clone.table), custom_call_target="tpu_custom_call" | custom-call | tf_op jit(solution)/shard_map/pallas_call | solution.py:670
  35.2 1.1 %shard_map.77 = (f32[16,256]{1,0:T(8,128)}, f32[16,256]{1,0:T(8,128)}, f32[8]{0:T(128)}) custom-call(f32[16,256]{1,0:T(8,128)S(1)} %get-tuple-element.6.resist, f32[16,256]{1,0:T(8,128)S(1)} %get-tuple-element.7.mask_grad, f32[1,128]{1,0:T(1,128)S(1)} %get-tuple-element.8.source_grad), custom_call_target="tpu_custom_call" | custom-call | tf_op jit(solution)/shard_map/pallas_call | solution.py:708

commit v6 on v5

--- a/solution.py
+++ b/solution.py
@@ -30,7 +30,8 @@
 QUAD = 4
 GROUP = 4
 DEPTH = 8
-HUB = 2 * GROUP
+HUB = 3 * GROUP
+RIDERS = (31, 63, 95)
 
 MESH = pl.DeviceIdType.MESH
 BF16 = ml_dtypes.bfloat16
@@ -70,7 +71,7 @@
     parts = {}
 
     real, imag = waves(np.arange(HALF), np.arange(EXT), EXT)
-    fwd = np.concatenate([real, -imag], axis=0).T / EXT
+    fwd = np.concatenate([real, -imag], axis=0).T
     wide = np.zeros((2 * TILE, 2 * HALF))
     wide[:TILE] = fwd[MARGIN : MARGIN + TILE]
     wide[TILE + 96 : TILE + 128] = fwd[:MARGIN]
@@ -81,8 +82,7 @@
     rows = np.arange(TILE).reshape(N_SRC, 2, 8)
     first, second = rows[:, 0].reshape(-1), rows[:, 1].reshape(-1)
     real, imag = waves(row_freq, pixels, EXT)
-    real, imag = real / EXT, -imag / EXT
-    both = np.concatenate([real, imag], axis=0)
+    both = np.concatenate([real, -imag], axis=0)
     high, low = halves(np.concatenate([both[:, first], both[:, second]], axis=0))
     parts["spec"] = np.concatenate([high, high], axis=1)
     spec_low = low
@@ -97,7 +97,7 @@
         )
         high, low = halves(cols)
         parts["cols_" + name] = np.concatenate([high, high], axis=0)
-        parts["cols_low_" + name] = low
+        parts["cols_low_" + name] = np.concatenate([low, high], axis=0)
         high, low = halves(np.concatenate([cols[:, :COLS_C].T, cols[:, COLS_C:].T], axis=0))
         parts["cols_back_" + name] = np.concatenate([high, low], axis=1)
 
@@ -129,6 +129,10 @@
     parts["coarse_rows"] = high
     parts["coarse_rows_low"] = low
 
+    owners = [
+        side * DEPTH + (quad * QUAD + k - 1) % DEPTH for side in range(2) for quad in range(2) for k in range(QUAD)
+    ]
+    first, second = rows[owners, 0].reshape(-1), rows[owners, 1].reshape(-1)
     high, low = halves(np.concatenate([both[:, first], both[:, second]], axis=1).T)
     parts["leave"] = np.concatenate([high, high], axis=1)
     leave_low = low
@@ -192,14 +196,14 @@
     outer = (quarter == 0) | (quarter == 3)
     even = jnp.where(outer, both[:BAND], turned[:BAND])
     odd = jnp.where(outer, turned[BAND:], both[BAND:])
-    return jnp.where(quarter == 3, -even, even) + jnp.where(quarter == 0, -odd, odd)
+    return (jnp.where(quarter == 3, -even, even) + jnp.where(quarter == 0, -odd, odd)) * (1.0 / (EXT * EXT))
 
 
 def pupil_of(row_shift, col_shift):
-    row = lax.broadcasted_iota(jnp.int32, (BAND, 128), 0) - BAND // 2 + row_shift
+    row = (lax.broadcasted_iota(jnp.int32, (BAND, 128), 0) - BAND // 2).astype(jnp.float32) + row_shift
     slot = lanes((1, 128)) & 63
-    col = jnp.where(slot < HALF, slot, HALF - slot) + col_shift
-    room = jnp.where(slot == HALF, -1, RAD * RAD - col * col)
+    col = jnp.where(slot < HALF, slot, HALF - slot).astype(jnp.float32) + col_shift
+    room = jnp.where(slot == HALF, -1.0, RAD * RAD - col * col)
     return jnp.where(row * row <= room, 1.0, 0.0)
 
 
@@ -208,14 +212,18 @@
 
 
 def coarse_fields(spec, pupils, cols, rows):
-    high, low = cut(spec)
+    high = spec.astype(jnp.bfloat16)
+    rest = spec - high.astype(jnp.float32)
+    low, lowest = cut(rest)
     mids = []
     for which in range(2):
-        band_high = jnp.concatenate([high * pupil for pupil in pupils[which::2]], axis=0)
-        band_low = jnp.concatenate([low * pupil for pupil in pupils[which::2]], axis=0)
+        band_high, band_low, band_lowest = [
+            jnp.concatenate([part * pupil for pupil in pupils[which::2]], axis=0) for part in (high, low, lowest)
+        ]
         table, low_table = cols[which]
         mids.append(
-            dot(jnp.concatenate([band_high, band_low], axis=1), table) + dot(band_high, low_table)
+            dot(jnp.concatenate([band_high, band_low], axis=1), table)
+            + dot(jnp.concatenate([band_high, band_lowest], axis=1), low_table)
         )
     fields = []
     for group in range(2):
@@ -314,20 +322,18 @@
     first = lanes(total.shape) < 64
     value = jnp.concatenate([jnp.where(first, total, 0.0), jnp.where(first, 0.0, total)], axis=0)
     high, low = cut(value)
-    return dot(high, last) + dot(low, last) + dot(high, last_low)
+    return (dot(high, last) + dot(low, last) + dot(high, last_low)) * (1.0 / (EXT * EXT))
 
 
 def rank_of(side, along):
-    return 2 * jnp.where(along < DEPTH // 2, along, DEPTH + DEPTH // 2 - 1 - along) + side
+    step = jnp.where(along == 3, 4, jnp.where(along == 7, 3, 11 - along))
+    return 2 * jnp.where(along < 3, along, step) + side
 
 
 def src_of(rank):
     step, side = rank // 2, rank % 2
-    return side * DEPTH + jnp.where(step < DEPTH // 2, step, DEPTH + DEPTH // 2 - 1 - step)
-
-
-RANKED = tuple(side * DEPTH + along for along in (0, 1, 2, 3, 7, 6, 5, 4) for side in range(2))
-SERVED = tuple(range(0, N_SRC, 2)) + tuple(range(1, N_SRC, 2))
+    along = jnp.where(step == 3, 7, jnp.where(step == 4, 3, 11 - step))
+    return side * DEPTH + jnp.where(step < 3, step, along)
 
 
 def repeat(first, last, body):
@@ -350,14 +356,18 @@
     has_left, has_right = tile > 0, tile < n_tile - 1
     side, along = src // DEPTH, src % DEPTH
     rank = rank_of(side, along)
-    quad = along // QUAD
+    place_in_quad = (along + 1) % QUAD
+    quad = (along + 1) % DEPTH // QUAD
     partners = [
         (side + across) % 2 * DEPTH + (along + step) % DEPTH for across, step in ((0, QUAD), (1, 0), (1, QUAD))
     ]
-    members = [side * DEPTH + quad * QUAD + (along + k) % QUAD for k in range(1, QUAD)]
+
+    def member(k):
+        return side * DEPTH + (quad * QUAD + k + DEPTH - 1) % DEPTH
+
     layer = tile // GROUP
     place = tile % GROUP
-    is_hub, is_teller = tile < HUB, layer == 1
+    is_hub, is_teller = tile < HUB, layer == HUB // GROUP - 1
 
     def get(name, start=None, stop=None):
         at, size = PLACES[name]
@@ -419,6 +429,7 @@
 
     for k in (1, 2, 4, 5, 6):
         local[k].start()
+    repeat(0, rank, lambda k: signal(ready_sem.at[rank], {"src": src_of(k)}))
     term_v[:, POINTS_R // 2 :, :] = jnp.zeros((QUAD, (ROWS_C - POINTS_R) // 2, 128), jnp.float32)
 
     @pl.when(jnp.logical_not(has_left))
@@ -431,15 +442,18 @@
 
     local[1].wait()
     local[2].wait()
-    spec_v[src, 8:16, :] = jnp.zeros((8, 128), jnp.float32)
-    spec_v[src, 8:10, 0:PER_DEV] = shifts_v[...].astype(jnp.float32)
-    spec_v[src, 10:11, 0:PER_DEV] = weights_v[...]
+    shape = (PER_DEV, PER_DEV)
+    own_place = lanes(shape) == lax.broadcasted_iota(jnp.int32, shape, 0)
+
+    def upright(row):
+        return jnp.sum(jnp.where(own_place, row, 0.0), axis=1, keepdims=True)
+
+    own_shifts = shifts_v[...].astype(jnp.float32)
+    riders = [upright(own_shifts[0:1, :]), upright(own_shifts[1:2, :]), upright(weights_v[...])]
     local[0].wait()
     local[3].wait()
     at = PLACES["enter"][0]
     own = enter(mask_v[...], table_v[at : at + TILE, :])
-    for k in SERVED:
-        pl.when(k < rank)(functools.partial(signal, ready_sem.at[rank], {"src": RANKED[k]}))
 
     @pl.when(has_left)
     def _():
@@ -451,30 +465,31 @@
 
     margins = jnp.concatenate([left_v[...], right_v[...]], axis=1)
     own = own + enter(margins, table_v[at + TILE : at + 2 * TILE, :])
-    spec_v[src, 0:8, :] = pack(own[:8], own[8:])
-    piece = pl.ds(0, 11)
+    own = pack(own[:8], own[8:])
+    for lane, rider in zip(RIDERS, riders):
+        own = jnp.where(lanes(own.shape) == lane, rider, own)
+    spec_v[src] = own
 
     def send_piece(k):
-        send(spec_v.at[src, piece], spec_v.at[src, piece], 2, {"src": RANKED[k]})
+        send(spec_v.at[src], spec_v.at[src], 2, {"src": src_of(k)})
 
     def answer_piece(k):
         pl.semaphore_wait(ready_sem.at[k], 1)
         send_piece(k)
 
-    for k in SERVED:
-        pl.when(k < rank)(functools.partial(send_piece, k))
-    for k in range(1, N_SRC):
-        pl.when(k > rank)(functools.partial(answer_piece, k))
+    repeat(0, (rank + 1) // 2, lambda k: send_piece(2 * k))
+    repeat(0, rank // 2, lambda k: send_piece(2 * k + 1))
+    repeat(rank + 1, N_SRC, answer_piece)
     repeat(0, jnp.where(is_hub, tile, 0), lambda k: signal(hub_sem.at[0], {"tile": k}))
 
     @pl.when(jnp.logical_not(is_hub))
     def _():
-        signal(hub_sem.at[1], {"tile": GROUP + place})
+        signal(hub_sem.at[1], {"tile": HUB - GROUP + place})
 
     local[4].wait()
-    wait(spec_v.at[pl.ds(0, N_SRC - 1), piece], recv_sem.at[2])
-
-    gathered = spec_v[:, 0:8, :].reshape(128, 128)
+    wait(spec_v.at[pl.ds(0, N_SRC - 1)], recv_sem.at[2])
+
+    gathered = spec_v[...].reshape(128, 128)
     spec = spectrum(gathered, get("spec"), get("lows_a", 0, 128), pltpu.roll)
     at = PLACES["lows_b"][0]
     cols = [(get("cols_" + name), get("cols_low_" + name)) for name in ("even", "odd")]
@@ -487,14 +502,11 @@
         owner = src
         for k, peer in enumerate(partners):
             owner = jnp.where(part == k + 1, peer, owner)
-        extra = spec_v[owner, 8:16, :]
-        shift = extra[0:2, :].astype(jnp.int32)
+        rows_by, cols_by, scales = [spec_v[owner, :, lane : lane + 1] for lane in RIDERS]
         for s in range(PER_DEV):
-            pupil_v[part, s] = pupil_of(shift[0:1, s : s + 1], shift[1:2, s : s + 1])
+            pupil_v[part, s] = pupil_of(rows_by[s : s + 1], cols_by[s : s + 1])
         for pair in range(PER_DEV // 2):
-            first, second = [
-                jnp.broadcast_to(extra[2:3, s : s + 1], (8, 128)) for s in (2 * pair, 2 * pair + 1)
-            ]
+            first, second = [jnp.broadcast_to(scales[s : s + 1], (8, 128)) for s in (2 * pair, 2 * pair + 1)]
             at = slice(128 * (pair % 2), 128 * (pair % 2) + 128)
             for parity, scale in enumerate(swap(first, second)):
                 scale_v[part, pair // 2, parity, :, at] = scale
@@ -513,15 +525,14 @@
 
     none = jnp.zeros((ROWS_C // 2, 128), jnp.float32)
     image = lax.fori_loop(0, QUAD, add_fields, (none, none), unroll=True)
-    place_in_quad = along % QUAD
     term_v[place_in_quad] = join_image(*image, pltpu.roll)
     image_rows = pl.ds(0, POINTS_R // 2)
     mine = term_v.at[place_in_quad, image_rows]
 
     def send_image(k):
-        send(mine, mine, 3, {"src": side * DEPTH + quad * QUAD + k})
-
-    for k in range(QUAD):
+        send(mine, mine, 3, {"src": member(k)})
+
+    for k in (1, 0, 2, 3):
         pl.when(k != place_in_quad)(functools.partial(send_image, k))
     local[5].wait()
     local[6].wait()
@@ -581,8 +592,8 @@
         return band_grad(total, adjoints, [pupil_v[part, s] for s in range(PER_DEV)], rows_back, cols_back)
 
     grad = lax.fori_loop(0, QUAD, add_part, jnp.zeros((BAND, 128), jnp.float32))
-    first = PLACES["leave"][0] + 8 * QUAD * (src // QUAD)
-    low_first = PLACES["lows_b"][0] + 8 * QUAD * (src // QUAD)
+    first = PLACES["leave"][0] + 8 * QUAD * (2 * side + quad)
+    low_first = PLACES["lows_b"][0] + 8 * QUAD * (2 * side + quad)
 
     def halves_of(start, stop, begin):
         begin = pl.multiple_of(begin, 32)
@@ -593,9 +604,9 @@
 
     rows = row_grads(grad, halves_of(0, 256, first), halves_of(0, 128, low_first), pltpu.roll)
     grad_v[...] = rows.reshape(QUAD, 8, 128)
-    for k, peer in enumerate(members):
-        send(grad_v.at[peer % QUAD], part_v.at[k], 4, {"src": peer})
-
+    for k in range(1, QUAD):
+        other = (place_in_quad + k) % QUAD
+        send(grad_v.at[other], part_v.at[k - 1], 4, {"src": member(other)})
 
     @pl.when(tile < HUB - 1)
     def _():
@@ -603,7 +614,7 @@
         repeat(tile + 1, HUB, send_sums)
 
     wait(part_v, recv_sem.at[4])
-    total = grad_v[along % QUAD] + part_v[0] + part_v[1] + part_v[2]
+    total = grad_v[place_in_quad] + part_v[0] + part_v[1] + part_v[2]
     mask_grad[...] = last_step(total, get("last"), get("last_low"))
 
     @pl.when(is_hub)
@@ -616,8 +627,8 @@
 
     @pl.when(is_teller)
     def _():
-        pl.semaphore_wait(hub_sem.at[1], n_tile // GROUP - 2)
-        repeat(2, n_tile // GROUP, tell)
+        pl.semaphore_wait(hub_sem.at[1], (n_tile - HUB) // GROUP)
+        repeat(HUB // GROUP, n_tile // GROUP, tell)
 
     @pl.when(jnp.logical_not(is_hub))
     def _():
@@ -627,7 +638,7 @@
 
     @pl.when(is_teller)
     def _():
-        wait(sums_v.at[pl.ds(0, n_tile // GROUP - 2)], send_sem.at[6])
+        wait(sums_v.at[pl.ds(0, (n_tile - HUB) // GROUP)], send_sem.at[6])
 
     @pl.when(is_hub)
     def _():
@@ -646,19 +657,20 @@
     def _():
         wait(right_v, send_sem.at[1])
 
-    wait(spec_v.at[pl.ds(0, N_SRC - 1), piece], send_sem.at[2])
+    wait(spec_v.at[pl.ds(0, N_SRC - 1)], send_sem.at[2])
     wait(term_v.at[pl.ds(0, QUAD - 1), image_rows], send_sem.at[3])
     wait(part_v, send_sem.at[4])
 
 
-def hand_over(resist, mask_grad, source_grad, resist_out, mask_grad_out, source_grad_out, sem):
+def hand_over(resist, mask_grad, source_grad, resist_out, mask_grad_out, source_grad_out, row, sem):
+    row[...] = source_grad[0, :PER_DEV]
     copies = [
         pltpu.make_async_copy(resist, resist_out, sem.at[0]),
         pltpu.make_async_copy(mask_grad, mask_grad_out, sem.at[1]),
+        pltpu.make_async_copy(row, source_grad_out, sem.at[2]),
     ]
     for copy in copies:
         copy.start()
-    source_grad_out[...] = source_grad[0, :PER_DEV]
     for copy in copies:
         copy.wait()
 
@@ -684,7 +696,7 @@
             pltpu.VMEM(TABLE.shape, jnp.bfloat16),
             pltpu.VMEM((ROWS, 128), f32),
             pltpu.VMEM((ROWS, 128), f32),
-            pltpu.VMEM((N_SRC, 16, 128), f32),
+            pltpu.VMEM((N_SRC, 8, 128), f32),
             pltpu.VMEM((QUAD, PER_DEV, BAND, 128), f32),
             pltpu.VMEM((QUAD, 2, 2, 8, 256), f32),
             pltpu.VMEM((QUAD, ROWS_C // 2, 128), f32),
@@ -713,8 +725,8 @@
             jax.ShapeDtypeStruct((PER_DEV,), f32),
         ),
         in_specs=[inside] * 3,
-        out_specs=(anywhere, anywhere, inside),
-        scratch_shapes=[pltpu.SemaphoreType.DMA((2,))],
+        out_specs=(anywhere,) * 3,
+        scratch_shapes=[pltpu.VMEM((PER_DEV,), f32), pltpu.SemaphoreType.DMA((3,))],
     )(*[pltpu.with_memory_space_constraint(result, pltpu.VMEM) for result in results])
 
 

time: 37 us -> 36.1 us (0.976); the launches traced: 36.4 us -> 36 us
  Pallas kernels: 35.7 us -> 35.3 us
    pallas_call x1, Pallas kernels: 1.14 us -> 0.64 us  [local(): pl.pallas_call(hand_over, out_shape=(jax.ShapeDtypeStruct((ROWS, TILE), f...]
where the time goes in v6:
time: 36.1 us; the launch traced here: 36 us
  Pallas kernels  35.3 us (98%)
  between operations  0.64 us (2%)
    pallas_call x1, Pallas kernels, local(): pl.pallas_call(everything, out_shape=(pltpu.VMEM((ROWS, TILE), f32), pltp...  34.7 us

profile of v6, /device:TPU:1, one launch (start us, length us, event | category | flops | bytes accessed | tf_op | source)
XLA Modules:
  0.0 36.0 jit_solution(6753985540889393654)
XLA Ops:
  0.6 34.7 %shard_map.76 = (f32[16,256]{1,0:T(8,128)S(1)}, f32[16,256]{1,0:T(8,128)S(1)}, f32[1,128]{1,0:T(1,128)S(1)}) custom-call(f32[16,256]{1,0:T(8,128)} %mask.1, s32[256,256]{1,0:T(8,128)} %target.1, s32[2,8]{1,0:T(2,128)} %bitcast.2, f32[1,8]{1,0:T(1,128)} %bitcast.3, bf16[4800,256]{1,0:T(8,128)(2,1)} %constant.2.clone.table), custom_call_target="tpu_custom_call" | custom-call | tf_op jit(solution)/shard_map/pallas_call | solution.py:682
  35.3 0.6 %shard_map.77 = (f32[16,256]{1,0:T(8,128)}, f32[16,256]{1,0:T(8,128)}, f32[8]{0:T(128)}) custom-call(f32[16,256]{1,0:T(8,128)S(1)} %get-tuple-element.6.resist, f32[16,256]{1,0:T(8,128)S(1)} %get-tuple-element.7.mask_grad, f32[1,128]{1,0:T(1,128)S(1)} %get-tuple-element.8.source_grad), custom_call_target="tpu_custom_call" | custom-call | tf_op jit(solution)/shard_map/pallas_call | solution.py:720

commit v7 on v6

--- a/solution.py
+++ b/solution.py
@@ -96,8 +96,10 @@
             [np.concatenate([real, imag], axis=1), np.concatenate([-imag, real], axis=1)], axis=0
         )
         high, low = halves(cols)
-        parts["cols_" + name] = np.concatenate([high, high], axis=0)
-        parts["cols_low_" + name] = np.concatenate([low, high], axis=0)
+        again = high.copy()
+        again[[HALF, 3 * HALF]] = high[[0, 2 * HALF]]
+        parts["cols_" + name] = np.concatenate([high, again], axis=0)
+        parts["cols_low_" + name] = low
         high, low = halves(np.concatenate([cols[:, :COLS_C].T, cols[:, COLS_C:].T], axis=0))
         parts["cols_back_" + name] = np.concatenate([high, low], axis=1)
 
@@ -177,9 +179,9 @@
 
 
 def enter(value, table):
-    high, low = cut(value)
-    both = dot(high, table)
-    return both[:, :128] + both[:, 128:] + dot(low, table[:, :128])
+    rows = value.shape[0]
+    both = dot(jnp.concatenate(cut(value), axis=0), table)
+    return both[:rows, :128] + both[:rows, 128:] + both[rows:, :128]
 
 
 def pack(first, second):
@@ -203,7 +205,7 @@
     row = (lax.broadcasted_iota(jnp.int32, (BAND, 128), 0) - BAND // 2).astype(jnp.float32) + row_shift
     slot = lanes((1, 128)) & 63
     col = jnp.where(slot < HALF, slot, HALF - slot).astype(jnp.float32) + col_shift
-    room = jnp.where(slot == HALF, -1.0, RAD * RAD - col * col)
+    room = RAD * RAD - col * col
     return jnp.where(row * row <= room, 1.0, 0.0)
 
 
@@ -211,19 +213,24 @@
     return pack(first, second), pack(second, first)
 
 
-def coarse_fields(spec, pupils, cols, rows):
-    high = spec.astype(jnp.bfloat16)
-    rest = spec - high.astype(jnp.float32)
-    low, lowest = cut(rest)
+def split_bands(spec, roll):
+    spare = (lanes(spec.shape) & 63) == HALF
+    high, low = cut(jnp.where(spare, 0.0, spec))
+    left = spec - high.astype(jnp.float32) - low.astype(jnp.float32)
+    low = jnp.where(spare, roll(left, HALF, 1), low.astype(jnp.float32)).astype(jnp.bfloat16)
+    return high, low
+
+
+def coarse_fields(bands, pupils, cols, rows):
+    high, low = bands
     mids = []
     for which in range(2):
-        band_high, band_low, band_lowest = [
-            jnp.concatenate([part * pupil for pupil in pupils[which::2]], axis=0) for part in (high, low, lowest)
+        band_high, band_low = [
+            jnp.concatenate([part * pupil for pupil in pupils[which::2]], axis=0) for part in (high, low)
         ]
         table, low_table = cols[which]
         mids.append(
-            dot(jnp.concatenate([band_high, band_low], axis=1), table)
-            + dot(jnp.concatenate([band_high, band_lowest], axis=1), low_table)
+            dot(jnp.concatenate([band_high, band_low], axis=1), table) + dot(band_high, low_table)
         )
     fields = []
     for group in range(2):
@@ -491,6 +498,7 @@
 
     gathered = spec_v[...].reshape(128, 128)
     spec = spectrum(gathered, get("spec"), get("lows_a", 0, 128), pltpu.roll)
+    bands = split_bands(spec, pltpu.roll)
     at = PLACES["lows_b"][0]
     cols = [(get("cols_" + name), get("cols_low_" + name)) for name in ("even", "odd")]
     rows = [
@@ -511,7 +519,7 @@
             for parity, scale in enumerate(swap(first, second)):
                 scale_v[part, pair // 2, parity, :, at] = scale
         fields = coarse_fields(
-            spec, [pupil_v[part, s].astype(jnp.bfloat16) for s in range(PER_DEV)], cols, rows
+            bands, [pupil_v[part, s].astype(jnp.bfloat16) for s in range(PER_DEV)], cols, rows
         )
         images = list(images)
         for group in range(2):
@@ -545,8 +553,6 @@
         get("fine_cols_low"),
     )
     printed = jax.nn.sigmoid(STEEP * (image * (1.0 / SOURCES) - THRESH))
-    printed_v[...] = printed
-    resist[...] = printed_v[pl.ds(pl.multiple_of(src * ROWS, ROWS), ROWS), :]
     goal = target_v[...].astype(jnp.float32)
     slope = (LOSS_SCALE * 2.0 * STEEP) * (printed - goal) * printed * (1.0 - printed)
     coarse = coarse_of(slope, get("coarse_rows"), get("coarse_rows_low"), get("coarse_cols"))
@@ -577,6 +583,9 @@
     for k in range(HUB):
         first = k + 1 - 2 * (k % 2)
         pl.when(first < tile)(functools.partial(send_sums, first))
+
+    printed_v[...] = printed
+    resist[...] = printed_v[pl.ds(pl.multiple_of(src * ROWS, ROWS), ROWS), :]
 
     wide = [jnp.concatenate([slope, slope], axis=1) * (2.0 / SOURCES) for slope in slopes]
     rows_back = [get("rows_back_even"), get("rows_back_odd")]

time: 36.1 us -> 36 us (level)
  no operation moved by 1% of the time
where the time goes in v7:
time: 36 us; the launch traced here: 35.9 us
  Pallas kernels  35.2 us (98%)
  between operations  0.64 us (2%)
    pallas_call x1, Pallas kernels, local(): pl.pallas_call(everything, out_shape=(pltpu.VMEM((ROWS, TILE), f32), pltp...  34.6 us

profile of v7, /device:TPU:1, one launch (start us, length us, event | category | flops | bytes accessed | tf_op | source)
XLA Modules:
  0.0 35.9 jit_solution(11774852185123246545)
XLA Ops:
  0.6 34.6 %shard_map.76 = (f32[16,256]{1,0:T(8,128)S(1)}, f32[16,256]{1,0:T(8,128)S(1)}, f32[1,128]{1,0:T(1,128)S(1)}) custom-call(f32[16,256]{1,0:T(8,128)} %mask.1, s32[256,256]{1,0:T(8,128)} %target.1, s32[2,8]{1,0:T(2,128)} %bitcast.2, f32[1,8]{1,0:T(1,128)} %bitcast.3, bf16[4544,256]{1,0:T(8,128)(2,1)} %constant.2.clone.table), custom_call_target="tpu_custom_call" | custom-call | tf_op jit(solution)/shard_map/pallas_call | solution.py:691
  35.2 0.6 %shard_map.77 = (f32[16,256]{1,0:T(8,128)}, f32[16,256]{1,0:T(8,128)}, f32[8]{0:T(128)}) custom-call(f32[16,256]{1,0:T(8,128)S(1)} %get-tuple-element.6.resist, f32[16,256]{1,0:T(8,128)S(1)} %get-tuple-element.7.mask_grad, f32[1,128]{1,0:T(1,128)S(1)} %get-tuple-element.8.source_grad), custom_call_target="tpu_custom_call" | custom-call | tf_op jit(solution)/shard_map/pallas_call | solution.py:729

commit v8 on v7

--- a/solution.py
+++ b/solution.py
@@ -174,6 +174,16 @@
     return high, low
 
 
+def beside(value):
+    high, low = cut(value)
+    return jnp.concatenate([high, low, high], axis=1)
+
+
+def below(value):
+    high, low = cut(value)
+    return jnp.concatenate([high, low, high], axis=0)
+
+
 def lanes(shape):
     return lax.broadcasted_iota(jnp.int32, shape, 1)
 
@@ -189,8 +199,7 @@
 
 
 def spectrum(gathered, table, low_table, roll):
-    high, low = cut(gathered)
-    out = dot(table, jnp.concatenate([high, low], axis=0)) + dot(low_table, high)
+    out = dot(jnp.concatenate([table, low_table], axis=1), below(gathered))
     both = pack(out[:128], out[128:])
     both = both + roll(both, 64, 1)
     turned = roll(both, 32, 1)
@@ -228,10 +237,7 @@
         band_high, band_low = [
             jnp.concatenate([part * pupil for pupil in pupils[which::2]], axis=0) for part in (high, low)
         ]
-        table, low_table = cols[which]
-        mids.append(
-            dot(jnp.concatenate([band_high, band_low], axis=1), table) + dot(band_high, low_table)
-        )
+        mids.append(dot(jnp.concatenate([band_high, band_low, band_high], axis=1), cols[which]))
     fields = []
     for group in range(2):
         stacks = ([], [])
@@ -243,9 +249,7 @@
                 stacks[parity].append(jnp.concatenate([real[parity], imag[parity]], axis=0))
         both = []
         for parity in range(2):
-            upper, lower = cut(jnp.concatenate(stacks[parity], axis=1))
-            table, low_table = rows[parity]
-            both.append(dot(table, jnp.concatenate([upper, lower], axis=0)) + dot(low_table, upper))
+            both.append(dot(rows[parity], below(jnp.concatenate(stacks[parity], axis=1))))
         fields.append(both)
     return fields
 
@@ -259,12 +263,10 @@
     return pack(even + roll(even, 64, 1), odd + roll(odd, 64, 1))
 
 
-def pixels_of(coarse, fine_rows, fine_cols, fine_cols_low):
+def pixels_of(coarse, fine_rows, fine_cols):
     first = lanes(coarse.shape) < 64
     coarse = jnp.concatenate([jnp.where(first, coarse, 0.0), jnp.where(first, 0.0, coarse)], axis=0)
-    high, low = cut(coarse)
-    mid = dot(jnp.concatenate([high, low], axis=1), fine_cols) + dot(high, fine_cols_low)
-    return dot(fine_rows, three(mid))
+    return dot(fine_rows, three(dot(beside(coarse), fine_cols)))
 
 
 def three(value):
@@ -274,8 +276,7 @@
 
 
 def coarse_of(slope, coarse_rows, coarse_rows_low, coarse_cols):
-    high, low = cut(slope)
-    mid = dot(coarse_rows, high) + dot(coarse_rows, low) + dot(coarse_rows_low, high)
+    mid = dot(jnp.concatenate([coarse_rows, coarse_rows, coarse_rows_low], axis=1), below(slope))
     high, low = cut(mid)
     both = dot(high, coarse_cols)
     return both[:, :128] + both[:, 128:] + dot(low, coarse_cols[:, :128])
@@ -319,8 +320,7 @@
 
 
 def row_grads(grad, leave, leave_low, roll):
-    high, low = cut(fold(grad, roll))
-    out = dot(leave, jnp.concatenate([high, low], axis=0)) + dot(leave_low, high)
+    out = dot(jnp.concatenate([leave, leave_low], axis=1), below(fold(grad, roll)))
     half = out.shape[0] // 2
     return pack(out[:half], out[half:])
 
@@ -382,6 +382,10 @@
             return table_v[at : at + size, :]
         return table_v[at : at + size, start:stop]
 
+    def joint(name, last):
+        start, (at, size) = PLACES[name][0], PLACES[last]
+        return table_v[start : at + size, :]
+
     def signal(sem, device):
         pl.semaphore_signal(sem, inc=1, device_id=device, device_id_type=MESH)
 
@@ -500,10 +504,10 @@
     spec = spectrum(gathered, get("spec"), get("lows_a", 0, 128), pltpu.roll)
     bands = split_bands(spec, pltpu.roll)
     at = PLACES["lows_b"][0]
-    cols = [(get("cols_" + name), get("cols_low_" + name)) for name in ("even", "odd")]
+    cols = [joint("cols_" + name, "cols_low_" + name) for name in ("even", "odd")]
     rows = [
-        (get("rows_even"), table_v[at : at + ROWS_C, 128:256]),
-        (get("rows_odd"), table_v[at + ROWS_C : at + 2 * ROWS_C, 128:256]),
+        jnp.concatenate([get("rows_even"), table_v[at : at + ROWS_C, 128:256]], axis=1),
+        jnp.concatenate([get("rows_odd"), table_v[at + ROWS_C : at + 2 * ROWS_C, 128:256]], axis=1),
     ]
 
     def add_fields(part, images):
@@ -549,8 +553,7 @@
     image = pixels_of(
         term_v[0] + term_v[1] + term_v[2] + term_v[3],
         get("fine_rows"),
-        get("fine_cols"),
-        get("fine_cols_low"),
+        joint("fine_cols", "fine_cols_low"),
     )
     printed = jax.nn.sigmoid(STEEP * (image * (1.0 / SOURCES) - THRESH))
     goal = target_v[...].astype(jnp.float32)

time: 36 us -> 36.1 us (level)
  no operation moved by 1% of the time
where the time goes in v8:
time: 36.1 us; the launch traced here: 36 us
  Pallas kernels  35.3 us (98%)
  between operations  0.64 us (2%)
    pallas_call x1, Pallas kernels, local(): pl.pallas_call(everything, out_shape=(pltpu.VMEM((ROWS, TILE), f32), pltp...  34.7 us

profile of v8, /device:TPU:1, one launch (start us, length us, event | category | flops | bytes accessed | tf_op | source)
XLA Modules:
  0.0 36.0 jit_solution(8837695692975486819)
XLA Ops:
  0.6 34.7 %shard_map.76 = (f32[16,256]{1,0:T(8,128)S(1)}, f32[16,256]{1,0:T(8,128)S(1)}, f32[1,128]{1,0:T(1,128)S(1)}) custom-call(f32[16,256]{1,0:T(8,128)} %mask.1, s32[256,256]{1,0:T(8,128)} %target.1, s32[2,8]{1,0:T(2,128)} %bitcast.2, f32[1,8]{1,0:T(1,128)} %bitcast.3, bf16[4544,256]{1,0:T(8,128)(2,1)} %constant.2.clone.table), custom_call_target="tpu_custom_call" | custom-call | tf_op jit(solution)/shard_map/pallas_call | solution.py:694
  35.3 0.6 %shard_map.77 = (f32[16,256]{1,0:T(8,128)}, f32[16,256]{1,0:T(8,128)}, f32[8]{0:T(128)}) custom-call(f32[16,256]{1,0:T(8,128)S(1)} %get-tuple-element.6.resist, f32[16,256]{1,0:T(8,128)S(1)} %get-tuple-element.7.mask_grad, f32[1,128]{1,0:T(1,128)S(1)} %get-tuple-element.8.source_grad), custom_call_target="tpu_custom_call" | custom-call | tf_op jit(solution)/shard_map/pallas_call | solution.py:732

commit v9 on v7

--- a/solution.py
+++ b/solution.py
@@ -32,6 +32,7 @@
 DEPTH = 8
 HUB = 3 * GROUP
 RIDERS = (31, 63, 95)
+RELAYS = (0, 8, 6, 14)
 
 MESH = pl.DeviceIdType.MESH
 BF16 = ml_dtypes.bfloat16
@@ -354,7 +355,7 @@
 def everything(mask, target, shifts, weights, table, resist, mask_grad, source_grad, *scratch):
     (
         mask_v, target_v, shifts_v, weights_v, table_v,
-        left_v, right_v, spec_v, pupil_v, scale_v, term_v, field_v, power_v,
+        edge_v, margin_v, spec_v, pupil_v, scale_v, term_v, field_v, power_v,
         printed_v, grad_v, part_v, sums_v, total_v, local_sem, send_sem, recv_sem, ready_sem, hub_sem,
     ) = scratch
     tile, src = lax.axis_index("tile"), lax.axis_index("src")
@@ -374,6 +375,7 @@
 
     layer = tile // GROUP
     place = tile % GROUP
+    is_relay = functools.reduce(jnp.logical_or, [src == relay for relay in RELAYS])
     is_hub, is_teller = tile < HUB, layer == HUB // GROUP - 1
 
     def get(name, start=None, stop=None):
@@ -400,15 +402,6 @@
         pltpu.make_async_copy(ref, ref, sem).wait()
 
     barrier = pltpu.get_barrier_semaphore()
-
-    @pl.when(has_left)
-    def _():
-        signal(barrier, {"tile": left})
-
-    @pl.when(has_right)
-    def _():
-        signal(barrier, {"tile": right})
-
     repeat(rank + 1, N_SRC, lambda k: signal(barrier, {"src": src_of(k)}))
     local = [
         pltpu.make_async_copy(mask, mask_v, local_sem.at[0]),
@@ -423,29 +416,26 @@
     local[3].start()
     repeat(jnp.where(is_hub, tile + 1, n_tile), n_tile, lambda k: signal(barrier, {"tile": k}))
 
+
+    @pl.when(is_relay)
+    def _():
+        pl.when(has_left)(lambda: repeat(0, N_SRC, lambda k: signal(barrier, {"tile": left, "src": k})))
+        pl.when(has_right)(lambda: repeat(0, N_SRC, lambda k: signal(barrier, {"tile": right, "src": k})))
+
     ends = has_left.astype(jnp.int32) + has_right.astype(jnp.int32)
-    pl.semaphore_wait(barrier, rank + ends + jnp.minimum(tile, HUB))
-
-    @pl.when(has_right)
-    def _():
-        send(mask.at[:, pl.ds(128, 128)], left_v, 0, {"tile": right})
-
-    @pl.when(has_left)
-    def _():
-        send(mask.at[:, pl.ds(0, 128)], right_v, 1, {"tile": left})
-
+    pl.semaphore_wait(barrier, rank + len(RELAYS) * ends + jnp.minimum(tile, HUB))
+
+    def send_edge(number, relay):
+        here = mask.at[:, pl.ds(128 - 128 * number, 128)]
+        send(here, edge_v.at[number, src], number, {"tile": (right, left)[number], "src": relay})
+
+    for relay in RELAYS:
+        pl.when(has_right)(functools.partial(send_edge, 0, relay))
+        pl.when(has_left)(functools.partial(send_edge, 1, relay))
     for k in (1, 2, 4, 5, 6):
         local[k].start()
     repeat(0, rank, lambda k: signal(ready_sem.at[rank], {"src": src_of(k)}))
     term_v[:, POINTS_R // 2 :, :] = jnp.zeros((QUAD, (ROWS_C - POINTS_R) // 2, 128), jnp.float32)
-
-    @pl.when(jnp.logical_not(has_left))
-    def _():
-        left_v[...] = jnp.zeros_like(left_v)
-
-    @pl.when(jnp.logical_not(has_right))
-    def _():
-        right_v[...] = jnp.zeros_like(right_v)
 
     local[1].wait()
     local[2].wait()
@@ -461,17 +451,6 @@
     local[3].wait()
     at = PLACES["enter"][0]
     own = enter(mask_v[...], table_v[at : at + TILE, :])
-
-    @pl.when(has_left)
-    def _():
-        wait(left_v, recv_sem.at[0])
-
-    @pl.when(has_right)
-    def _():
-        wait(right_v, recv_sem.at[1])
-
-    margins = jnp.concatenate([left_v[...], right_v[...]], axis=1)
-    own = own + enter(margins, table_v[at + TILE : at + 2 * TILE, :])
     own = pack(own[:8], own[8:])
     for lane, rider in zip(RIDERS, riders):
         own = jnp.where(lanes(own.shape) == lane, rider, own)
@@ -494,11 +473,37 @@
         signal(hub_sem.at[1], {"tile": HUB - GROUP + place})
 
     local[4].wait()
+    spec_tables = (get("spec"), get("lows_a", 0, 128))
+
+    @pl.when(is_relay)
+    def _():
+        for number, there in enumerate((has_left, has_right)):
+            pl.when(there)(functools.partial(wait, edge_v.at[number], recv_sem.at[number]))
+
+            @pl.when(jnp.logical_not(there))
+            def _():
+                edge_v[number] = jnp.zeros((N_SRC, ROWS, 128), jnp.float32)
+
+        sides = jnp.concatenate([edge_v[number].reshape(TILE, 128) for number in range(2)], axis=1)
+        margins = enter(sides, table_v[at + TILE : at + 2 * TILE, :]).reshape(N_SRC, 2, 8, 128)
+        margins = pack(margins[:, 0].reshape(128, 128), margins[:, 1].reshape(128, 128))
+        margin_v[...] = spectrum(margins, *spec_tables, pltpu.roll)
+        for k in range(QUAD):
+
+            @pl.when(k != place_in_quad)
+            def _():
+                send(margin_v, margin_v, 7, {"src": member(k)})
+
     wait(spec_v.at[pl.ds(0, N_SRC - 1)], recv_sem.at[2])
 
     gathered = spec_v[...].reshape(128, 128)
-    spec = spectrum(gathered, get("spec"), get("lows_a", 0, 128), pltpu.roll)
-    bands = split_bands(spec, pltpu.roll)
+    spec = spectrum(gathered, *spec_tables, pltpu.roll)
+
+    @pl.when(jnp.logical_not(is_relay))
+    def _():
+        wait(margin_v, recv_sem.at[7])
+
+    bands = split_bands(spec + margin_v[...], pltpu.roll)
     at = PLACES["lows_b"][0]
     cols = [(get("cols_" + name), get("cols_low_" + name)) for name in ("even", "odd")]
     rows = [
@@ -658,13 +663,13 @@
         wait(sums_v.at[pl.ds(0, HUB)], send_sem.at[5])
 
 
-    @pl.when(has_right)
-    def _():
-        wait(left_v, send_sem.at[0])
-
-    @pl.when(has_left)
-    def _():
-        wait(right_v, send_sem.at[1])
+    for number, there in enumerate((has_right, has_left)):
+        pl.when(there)(functools.partial(wait, edge_v.at[number, pl.ds(0, len(RELAYS))], send_sem.at[number]))
+
+    @pl.when(is_relay)
+    def _():
+        for _ in range(QUAD - 1):
+            wait(margin_v, send_sem.at[7])
 
     wait(spec_v.at[pl.ds(0, N_SRC - 1)], send_sem.at[2])
     wait(term_v.at[pl.ds(0, QUAD - 1), image_rows], send_sem.at[3])
@@ -703,8 +708,8 @@
             pltpu.VMEM((2, PER_DEV), jnp.int32),
             pltpu.VMEM((1, PER_DEV), f32),
             pltpu.VMEM(TABLE.shape, jnp.bfloat16),
-            pltpu.VMEM((ROWS, 128), f32),
-            pltpu.VMEM((ROWS, 128), f32),
+            pltpu.VMEM((2, N_SRC, ROWS, 128), f32),
+            pltpu.VMEM((BAND, 128), f32),
             pltpu.VMEM((N_SRC, 8, 128), f32),
             pltpu.VMEM((QUAD, PER_DEV, BAND, 128), f32),
             pltpu.VMEM((QUAD, 2, 2, 8, 256), f32),
@@ -717,8 +722,8 @@
             pltpu.VMEM((N_TILE, 1, 128), f32),
             pltpu.VMEM((1, 128), f32),
             pltpu.SemaphoreType.DMA((7,)),
-            pltpu.SemaphoreType.DMA((7,)),
-            pltpu.SemaphoreType.DMA((7,)),
+            pltpu.SemaphoreType.DMA((8,)),
+            pltpu.SemaphoreType.DMA((8,)),
             pltpu.SemaphoreType.REGULAR((N_SRC,)),
             pltpu.SemaphoreType.REGULAR((2,)),
         ],

time: 36 us -> 39 us (1.083)
  the two profiles are of different devices: /device:TPU:1 before, /device:TPU:52 now
where the time goes in v9:
time: 39 us; the launch traced here: 38.8 us
  Pallas kernels  38.2 us (98%)
  between operations  0.64 us (2%)
    pallas_call x1, Pallas kernels, local(): pl.pallas_call(everything, out_shape=(pltpu.VMEM((ROWS, TILE), f32), pltp...  37.5 us

profile of v9, /device:TPU:52, one launch (start us, length us, event | category | flops | bytes accessed | tf_op | source)
XLA Modules:
  0.0 38.8 jit_solution(9603492723476285720)
XLA Ops:
  0.6 37.5 %shard_map.76 = (f32[16,256]{1,0:T(8,128)S(1)}, f32[16,256]{1,0:T(8,128)S(1)}, f32[1,128]{1,0:T(1,128)S(1)}) custom-call(f32[16,256]{1,0:T(8,128)} %mask.1, s32[256,256]{1,0:T(8,128)} %target.1, s32[2,8]{1,0:T(2,128)} %bitcast.2, f32[1,8]{1,0:T(1,128)} %bitcast.3, bf16[4544,256]{1,0:T(8,128)(2,1)} %constant.2.clone.table), custom_call_target="tpu_custom_call" | custom-call | tf_op jit(solution)/shard_map/pallas_call | solution.py:696
  38.2 0.6 %shard_map.77 = (f32[16,256]{1,0:T(8,128)}, f32[16,256]{1,0:T(8,128)}, f32[8]{0:T(128)}) custom-call(f32[16,256]{1,0:T(8,128)S(1)} %get-tuple-element.6.resist, f32[16,256]{1,0:T(8,128)S(1)} %get-tuple-element.7.mask_grad, f32[1,128]{1,0:T(1,128)S(1)} %get-tuple-element.8.source_grad), custom_call_target="tpu_custom_call" | custom-call | tf_op jit(solution)/shard_map/pallas_call | solution.py:734

commit v10 on v7

--- a/solution.py
+++ b/solution.py
@@ -419,8 +419,8 @@
         rows = pl.ds(CUTS[k], CUTS[k + 1] - CUTS[k])
         local.append(pltpu.make_async_copy(table.at[rows], table_v.at[rows], local_sem.at[3 + k]))
     local.append(pltpu.make_async_copy(target, target_v, local_sem.at[6]))
-    local[0].start()
-    local[3].start()
+    for k in (0, 3, 1, 2):
+        local[k].start()
     repeat(jnp.where(is_hub, tile + 1, n_tile), n_tile, lambda k: signal(barrier, {"tile": k}))
 
     ends = has_left.astype(jnp.int32) + has_right.astype(jnp.int32)
@@ -434,8 +434,6 @@
     def _():
         send(mask.at[:, pl.ds(0, 128)], right_v, 1, {"tile": left})
 
-    for k in (1, 2, 4, 5, 6):
-        local[k].start()
     repeat(0, rank, lambda k: signal(ready_sem.at[rank], {"src": src_of(k)}))
     term_v[:, POINTS_R // 2 :, :] = jnp.zeros((QUAD, (ROWS_C - POINTS_R) // 2, 128), jnp.float32)
 
@@ -486,6 +484,8 @@
 
     repeat(0, (rank + 1) // 2, lambda k: send_piece(2 * k))
     repeat(0, rank // 2, lambda k: send_piece(2 * k + 1))
+    for k in (4, 5, 6):
+        local[k].start()
     repeat(rank + 1, N_SRC, answer_piece)
     repeat(0, jnp.where(is_hub, tile, 0), lambda k: signal(hub_sem.at[0], {"tile": k}))
 

time: 36 us -> 36 us (level)
  no operation moved by 1% of the time
where the time goes in v10:
time: 36 us; the launch traced here: 35.7 us
  Pallas kernels  35 us (97%)
  between operations  0.64 us (2%)
    pallas_call x1, Pallas kernels, local(): pl.pallas_call(everything, out_shape=(pltpu.VMEM((ROWS, TILE), f32), pltp...  34.4 us

profile of v10, /device:TPU:1, one launch (start us, length us, event | category | flops | bytes accessed | tf_op | source)
XLA Modules:
  0.0 35.7 jit_solution(12508875696914612011)
XLA Ops:
  0.6 34.4 %shard_map.76 = (f32[16,256]{1,0:T(8,128)S(1)}, f32[16,256]{1,0:T(8,128)S(1)}, f32[1,128]{1,0:T(1,128)S(1)}) custom-call(f32[16,256]{1,0:T(8,128)} %mask.1, s32[256,256]{1,0:T(8,128)} %target.1, s32[2,8]{1,0:T(2,128)} %bitcast.2, f32[1,8]{1,0:T(1,128)} %bitcast.3, bf16[4544,256]{1,0:T(8,128)(2,1)} %constant.2.clone.table), custom_call_target="tpu_custom_call" | custom-call | tf_op jit(solution)/shard_map/pallas_call | solution.py:691
  35.0 0.6 %shard_map.77 = (f32[16,256]{1,0:T(8,128)}, f32[16,256]{1,0:T(8,128)}, f32[8]{0:T(128)}) custom-call(f32[16,256]{1,0:T(8,128)S(1)} %get-tuple-element.6.resist, f32[16,256]{1,0:T(8,128)S(1)} %get-tuple-element.7.mask_grad, f32[1,128]{1,0:T(1,128)S(1)} %get-tuple-element.8.source_grad), custom_call_target="tpu_custom_call" | custom-call | tf_op jit(solution)/shard_map/pallas_call | solution.py:729

commit v11 on v7

--- a/solution.py
+++ b/solution.py
@@ -507,32 +507,32 @@
     ]
 
     def add_fields(part, images):
-        owner = src
-        for k, peer in enumerate(partners):
-            owner = jnp.where(part == k + 1, peer, owner)
+        owner = ([src] + partners)[part]
         rows_by, cols_by, scales = [spec_v[owner, :, lane : lane + 1] for lane in RIDERS]
-        for s in range(PER_DEV):
-            pupil_v[part, s] = pupil_of(rows_by[s : s + 1], cols_by[s : s + 1])
+        pupils = [pupil_of(rows_by[s : s + 1], cols_by[s : s + 1]) for s in range(PER_DEV)]
         for pair in range(PER_DEV // 2):
             first, second = [jnp.broadcast_to(scales[s : s + 1], (8, 128)) for s in (2 * pair, 2 * pair + 1)]
             at = slice(128 * (pair % 2), 128 * (pair % 2) + 128)
             for parity, scale in enumerate(swap(first, second)):
                 scale_v[part, pair // 2, parity, :, at] = scale
-        fields = coarse_fields(
-            bands, [pupil_v[part, s].astype(jnp.bfloat16) for s in range(PER_DEV)], cols, rows
-        )
+        fields = coarse_fields(bands, [pupil.astype(jnp.bfloat16) for pupil in pupils], cols, rows)
+        for s, pupil in enumerate(pupils):
+            pupil_v[part, s] = pupil
         images = list(images)
         for group in range(2):
             for parity in range(2):
                 field_v[part, group, parity] = fields[group][parity]
                 power = power_of(fields[group][parity])
-                power_v[part, group, parity] = power
+                if part == 0:
+                    power_v[group, parity] = power
                 power = power * scale_v[part, group, parity, 0:1, :]
                 images[parity] = images[parity] + power[:, :128] + power[:, 128:]
         return tuple(images)
 
     none = jnp.zeros((ROWS_C // 2, 128), jnp.float32)
-    image = lax.fori_loop(0, QUAD, add_fields, (none, none), unroll=True)
+    image = (none, none)
+    for part in range(QUAD):
+        image = add_fields(part, image)
     term_v[place_in_quad] = join_image(*image, pltpu.roll)
     image_rows = pl.ds(0, POINTS_R // 2)
     mine = term_v.at[place_in_quad, image_rows]
@@ -562,7 +562,7 @@
     for pair in range(PER_DEV // 2):
         at = slice(128 * (pair % 2), 128 * (pair % 2) + 128)
         terms = [
-            jnp.sum(slopes[parity] * power_v[0, pair // 2, parity, :, at], axis=0, keepdims=True) for parity in range(2)
+            jnp.sum(slopes[parity] * power_v[pair // 2, parity, :, at], axis=0, keepdims=True) for parity in range(2)
         ]
         sums.extend(swap(*terms))
     sums = jnp.sum(jnp.concatenate(sums, axis=0), axis=1, keepdims=True)
@@ -710,7 +710,7 @@
             pltpu.VMEM((QUAD, 2, 2, 8, 256), f32),
             pltpu.VMEM((QUAD, ROWS_C // 2, 128), f32),
             pltpu.VMEM((QUAD, 2, 2, ROWS_C, 256), f32),
-            pltpu.VMEM((QUAD, 2, 2, ROWS_C // 2, 256), f32),
+            pltpu.VMEM((2, 2, ROWS_C // 2, 256), f32),
             pltpu.VMEM((TILE, TILE), f32),
             pltpu.VMEM((QUAD, 8, 128), f32),
             pltpu.VMEM((QUAD - 1, 8, 128), f32),

time: 36 us -> 36 us (level)
  no operation moved by 1% of the time
where the time goes in v11:
time: 36 us; the launch traced here: 35.8 us
  Pallas kernels  35.2 us (98%)
  between operations  0.64 us (2%)
    pallas_call x1, Pallas kernels, local(): pl.pallas_call(everything, out_shape=(pltpu.VMEM((ROWS, TILE), f32), pltp...  34.6 us

profile of v11, /device:TPU:1, one launch (start us, length us, event | category | flops | bytes accessed | tf_op | source)
XLA Modules:
  0.0 35.8 jit_solution(15284583753976368462)
XLA Ops:
  0.6 34.6 %shard_map.76 = (f32[16,256]{1,0:T(8,128)S(1)}, f32[16,256]{1,0:T(8,128)S(1)}, f32[1,128]{1,0:T(1,128)S(1)}) custom-call(f32[16,256]{1,0:T(8,128)} %mask.1, s32[256,256]{1,0:T(8,128)} %target.1, s32[2,8]{1,0:T(2,128)} %bitcast.2, f32[1,8]{1,0:T(1,128)} %bitcast.3, bf16[4544,256]{1,0:T(8,128)(2,1)} %constant.2.clone.table), custom_call_target="tpu_custom_call" | custom-call | tf_op jit(solution)/shard_map/pallas_call | solution.py:691
  35.2 0.6 %shard_map.77 = (f32[16,256]{1,0:T(8,128)}, f32[16,256]{1,0:T(8,128)}, f32[8]{0:T(128)}) custom-call(f32[16,256]{1,0:T(8,128)S(1)} %get-tuple-element.6.resist, f32[16,256]{1,0:T(8,128)S(1)} %get-tuple-element.7.mask_grad, f32[1,128]{1,0:T(1,128)S(1)} %get-tuple-element.8.source_grad), custom_call_target="tpu_custom_call" | custom-call | tf_op jit(solution)/shard_map/pallas_call | solution.py:729

commit v12 on v7

--- a/solution.py
+++ b/solution.py
@@ -369,8 +369,8 @@
         (side + across) % 2 * DEPTH + (along + step) % DEPTH for across, step in ((0, QUAD), (1, 0), (1, QUAD))
     ]
 
-    def member(k):
-        return side * DEPTH + (quad * QUAD + k + DEPTH - 1) % DEPTH
+    def member(k, group=quad):
+        return side * DEPTH + (group * QUAD + k + DEPTH - 1) % DEPTH
 
     layer = tile // GROUP
     place = tile % GROUP
@@ -484,7 +484,10 @@
         pl.semaphore_wait(ready_sem.at[k], 1)
         send_piece(k)
 
-    repeat(0, (rank + 1) // 2, lambda k: send_piece(2 * k))
+    def send_even(k):
+        send_piece(2 * jnp.where((rank >= N_SRC // 2) & (k < QUAD), (k + 1) % QUAD, k))
+
+    repeat(0, (rank + 1) // 2, send_even)
     repeat(0, rank // 2, lambda k: send_piece(2 * k + 1))
     repeat(rank + 1, N_SRC, answer_piece)
     repeat(0, jnp.where(is_hub, tile, 0), lambda k: signal(hub_sem.at[0], {"tile": k}))
@@ -537,11 +540,16 @@
     image_rows = pl.ds(0, POINTS_R // 2)
     mine = term_v.at[place_in_quad, image_rows]
 
-    def send_image(k):
-        send(mine, mine, 3, {"src": member(k)})
+    middle = (place_in_quad == 1) | (place_in_quad == 2)
+    tells_own, tells_other = jnp.logical_not(middle & (quad == 1)), middle & (quad == 0)
+
+    def send_image(k, group):
+        send(mine, mine, 3, {"src": member(k, group)})
 
     for k in (1, 0, 2, 3):
-        pl.when(k != place_in_quad)(functools.partial(send_image, k))
+        pl.when(tells_own & (k != place_in_quad))(functools.partial(send_image, k, quad))
+    for k in (3, 0, 1, 2):
+        pl.when(tells_other & (k != place_in_quad))(functools.partial(send_image, k, 1))
     local[5].wait()
     local[6].wait()
     wait(term_v.at[pl.ds(0, QUAD - 1), image_rows], recv_sem.at[3])
@@ -667,7 +675,8 @@
         wait(right_v, send_sem.at[1])
 
     wait(spec_v.at[pl.ds(0, N_SRC - 1)], send_sem.at[2])
-    wait(term_v.at[pl.ds(0, QUAD - 1), image_rows], send_sem.at[3])
+    for told in (tells_own, tells_other):
+        pl.when(told)(lambda: wait(term_v.at[pl.ds(0, QUAD - 1), image_rows], send_sem.at[3]))
     wait(part_v, send_sem.at[4])
 
 

time: 36 us -> 36 us (level)
  no operation moved by 1% of the time
where the time goes in v12:
time: 36 us; the launch traced here: 35.7 us
  Pallas kernels  35.1 us (98%)
  between operations  0.64 us (2%)
    pallas_call x1, Pallas kernels, local(): pl.pallas_call(everything, out_shape=(pltpu.VMEM((ROWS, TILE), f32), pltp...  34.4 us

profile of v12, /device:TPU:1, one launch (start us, length us, event | category | flops | bytes accessed | tf_op | source)
XLA Modules:
  0.0 35.7 jit_solution(9710622768553130377)
XLA Ops:
  0.6 34.4 %shard_map.76 = (f32[16,256]{1,0:T(8,128)S(1)}, f32[16,256]{1,0:T(8,128)S(1)}, f32[1,128]{1,0:T(1,128)S(1)}) custom-call(f32[16,256]{1,0:T(8,128)} %mask.1, s32[256,256]{1,0:T(8,128)} %target.1, s32[2,8]{1,0:T(2,128)} %bitcast.2, f32[1,8]{1,0:T(1,128)} %bitcast.3, bf16[4544,256]{1,0:T(8,128)(2,1)} %constant.2.clone.table), custom_call_target="tpu_custom_call" | custom-call | tf_op jit(solution)/shard_map/pallas_call | solution.py:700
  35.1 0.6 %shard_map.77 = (f32[16,256]{1,0:T(8,128)}, f32[16,256]{1,0:T(8,128)}, f32[8]{0:T(128)}) custom-call(f32[16,256]{1,0:T(8,128)S(1)} %get-tuple-element.6.resist, f32[16,256]{1,0:T(8,128)S(1)} %get-tuple-element.7.mask_grad, f32[1,128]{1,0:T(1,128)S(1)} %get-tuple-element.8.source_grad), custom_call_target="tpu_custom_call" | custom-call | tf_op jit(solution)/shard_map/pallas_call | solution.py:738

commit v13 on v7

--- a/solution.py
+++ b/solution.py
@@ -484,7 +484,13 @@
         pl.semaphore_wait(ready_sem.at[k], 1)
         send_piece(k)
 
-    repeat(0, (rank + 1) // 2, lambda k: send_piece(2 * k))
+    def send_even(k):
+        served = k
+        for place_in_row, turn in enumerate((1, 2, 3, 5, 4, 0)):
+            served = jnp.where((k == place_in_row) & (rank >= 11), turn, served)
+        send_piece(2 * served)
+
+    repeat(0, (rank + 1) // 2, send_even)
     repeat(0, rank // 2, lambda k: send_piece(2 * k + 1))
     repeat(rank + 1, N_SRC, answer_piece)
     repeat(0, jnp.where(is_hub, tile, 0), lambda k: signal(hub_sem.at[0], {"tile": k}))

time: 36 us -> 36 us (level)
  no operation moved by 1% of the time
where the time goes in v13:
time: 36 us; the launch traced here: 35.8 us
  Pallas kernels  35.2 us (98%)
  between operations  0.64 us (2%)
    pallas_call x1, Pallas kernels, local(): pl.pallas_call(everything, out_shape=(pltpu.VMEM((ROWS, TILE), f32), pltp...  34.6 us

profile of v13, /device:TPU:1, one launch (start us, length us, event | category | flops | bytes accessed | tf_op | source)
XLA Modules:
  0.0 35.8 jit_solution(11065135328244196455)
XLA Ops:
  0.6 34.6 %shard_map.76 = (f32[16,256]{1,0:T(8,128)S(1)}, f32[16,256]{1,0:T(8,128)S(1)}, f32[1,128]{1,0:T(1,128)S(1)}) custom-call(f32[16,256]{1,0:T(8,128)} %mask.1, s32[256,256]{1,0:T(8,128)} %target.1, s32[2,8]{1,0:T(2,128)} %bitcast.2, f32[1,8]{1,0:T(1,128)} %bitcast.3, bf16[4544,256]{1,0:T(8,128)(2,1)} %constant.2.clone.table), custom_call_target="tpu_custom_call" | custom-call | tf_op jit(solution)/shard_map/pallas_call | solution.py:697
  35.2 0.6 %shard_map.77 = (f32[16,256]{1,0:T(8,128)}, f32[16,256]{1,0:T(8,128)}, f32[8]{0:T(128)}) custom-call(f32[16,256]{1,0:T(8,128)S(1)} %get-tuple-element.6.resist, f32[16,256]{1,0:T(8,128)S(1)} %get-tuple-element.7.mask_grad, f32[1,128]{1,0:T(1,128)S(1)} %get-tuple-element.8.source_grad), custom_call_target="tpu_custom_call" | custom-call | tf_op jit(solution)/shard_map/pallas_call | solution.py:735

commit v14 on v12

--- a/solution.py
+++ b/solution.py
@@ -419,8 +419,8 @@
         rows = pl.ds(CUTS[k], CUTS[k + 1] - CUTS[k])
         local.append(pltpu.make_async_copy(table.at[rows], table_v.at[rows], local_sem.at[3 + k]))
     local.append(pltpu.make_async_copy(target, target_v, local_sem.at[6]))
-    local[0].start()
-    local[3].start()
+    for k in (0, 3, 1, 2):
+        local[k].start()
     repeat(jnp.where(is_hub, tile + 1, n_tile), n_tile, lambda k: signal(barrier, {"tile": k}))
 
     ends = has_left.astype(jnp.int32) + has_right.astype(jnp.int32)
@@ -434,8 +434,6 @@
     def _():
         send(mask.at[:, pl.ds(0, 128)], right_v, 1, {"tile": left})
 
-    for k in (1, 2, 4, 5, 6):
-        local[k].start()
     repeat(0, rank, lambda k: signal(ready_sem.at[rank], {"src": src_of(k)}))
     term_v[:, POINTS_R // 2 :, :] = jnp.zeros((QUAD, (ROWS_C - POINTS_R) // 2, 128), jnp.float32)
 
@@ -489,6 +487,8 @@
 
     repeat(0, (rank + 1) // 2, send_even)
     repeat(0, rank // 2, lambda k: send_piece(2 * k + 1))
+    for k in (4, 5, 6):
+        local[k].start()
     repeat(rank + 1, N_SRC, answer_piece)
     repeat(0, jnp.where(is_hub, tile, 0), lambda k: signal(hub_sem.at[0], {"tile": k}))
 

time: 36 us -> 36 us (level)
  no operation moved by 1% of the time
where the time goes in v14:
time: 36 us; the launch traced here: 35.7 us
  Pallas kernels  35 us (97%)
  between operations  0.64 us (2%)
    pallas_call x1, Pallas kernels, local(): pl.pallas_call(everything, out_shape=(pltpu.VMEM((ROWS, TILE), f32), pltp...  34.4 us

profile of v14, /device:TPU:1, one launch (start us, length us, event | category | flops | bytes accessed | tf_op | source)
XLA Modules:
  0.0 35.7 jit_solution(7329685320404878585)
XLA Ops:
  0.6 34.4 %shard_map.76 = (f32[16,256]{1,0:T(8,128)S(1)}, f32[16,256]{1,0:T(8,128)S(1)}, f32[1,128]{1,0:T(1,128)S(1)}) custom-call(f32[16,256]{1,0:T(8,128)} %mask.1, s32[256,256]{1,0:T(8,128)} %target.1, s32[2,8]{1,0:T(2,128)} %bitcast.2, f32[1,8]{1,0:T(1,128)} %bitcast.3, bf16[4544,256]{1,0:T(8,128)(2,1)} %constant.2.clone.table), custom_call_target="tpu_custom_call" | custom-call | tf_op jit(solution)/shard_map/pallas_call | solution.py:700
  35.0 0.6 %shard_map.77 = (f32[16,256]{1,0:T(8,128)}, f32[16,256]{1,0:T(8,128)}, f32[8]{0:T(128)}) custom-call(f32[16,256]{1,0:T(8,128)S(1)} %get-tuple-element.6.resist, f32[16,256]{1,0:T(8,128)S(1)} %get-tuple-element.7.mask_grad, f32[1,128]{1,0:T(1,128)S(1)} %get-tuple-element.8.source_grad), custom_call_target="tpu_custom_call" | custom-call | tf_op jit(solution)/shard_map/pallas_call | solution.py:738

commit v15 on v7

--- a/solution.py
+++ b/solution.py
@@ -540,8 +540,9 @@
     def send_image(k):
         send(mine, mine, 3, {"src": member(k)})
 
-    for k in (1, 0, 2, 3):
-        pl.when(k != place_in_quad)(functools.partial(send_image, k))
+    for group, order in enumerate(((1, 0, 2, 3), (3, 0, 1, 2))):
+        for k in order:
+            pl.when((quad == group) & (k != place_in_quad))(functools.partial(send_image, k))
     local[5].wait()
     local[6].wait()
     wait(term_v.at[pl.ds(0, QUAD - 1), image_rows], recv_sem.at[3])

time: 36 us -> 36 us (level)
  no operation moved by 1% of the time
where the time goes in v15:
time: 36 us; the launch traced here: 35.9 us
  Pallas kernels  35.2 us (98%)
  between operations  0.64 us (2%)
    pallas_call x1, Pallas kernels, local(): pl.pallas_call(everything, out_shape=(pltpu.VMEM((ROWS, TILE), f32), pltp...  34.6 us

profile of v15, /device:TPU:1, one launch (start us, length us, event | category | flops | bytes accessed | tf_op | source)
XLA Modules:
  0.0 35.9 jit_solution(6434124349175839728)
XLA Ops:
  0.6 34.6 %shard_map.76 = (f32[16,256]{1,0:T(8,128)S(1)}, f32[16,256]{1,0:T(8,128)S(1)}, f32[1,128]{1,0:T(1,128)S(1)}) custom-call(f32[16,256]{1,0:T(8,128)} %mask.1, s32[256,256]{1,0:T(8,128)} %target.1, s32[2,8]{1,0:T(2,128)} %bitcast.2, f32[1,8]{1,0:T(1,128)} %bitcast.3, bf16[4544,256]{1,0:T(8,128)(2,1)} %constant.2.clone.table), custom_call_target="tpu_custom_call" | custom-call | tf_op jit(solution)/shard_map/pallas_call | solution.py:692
  35.2 0.6 %shard_map.77 = (f32[16,256]{1,0:T(8,128)}, f32[16,256]{1,0:T(8,128)}, f32[8]{0:T(128)}) custom-call(f32[16,256]{1,0:T(8,128)S(1)} %get-tuple-element.6.resist, f32[16,256]{1,0:T(8,128)S(1)} %get-tuple-element.7.mask_grad, f32[1,128]{1,0:T(1,128)S(1)} %get-tuple-element.8.source_grad), custom_call_target="tpu_custom_call" | custom-call | tf_op jit(solution)/shard_map/pallas_call | solution.py:730
